TPU v7x, 256 devices: a whole 4x4x8 slice. The times are simulated.
256 devices in a mesh: dp: 32 (over y, z), tp: 8 (over x, core).
Axes of the slice: x: 4, y: 4, z: 8, core: 2. Of those that a mesh axis runs over, the one named last changes fastest.
Arguments:
- queries: bfloat16 [512, 8192], P('dp', 'tp')
- fresh_token_key: bfloat16 [512, 1024], P('dp', 'tp')
- fresh_token_value: bfloat16 [512, 1024], P('dp', 'tp'), may hold values from -6 to 6
- key_value_pool: bfloat16 [20480, 2, 16, 1024], P('dp', None, None, 'tp'), may hold values from -6 to 6
- request_block_map: int32 [512, 32], P('dp'), may hold values from 0 to 639, as said below
- lengths: int32 [512], P('dp'), may hold values from 1 to 512, as said below
- row_counts: int32 [32], replicated, may hold values from 4 to 16, as said below
- move_src: int32 [32, 32, 4], replicated, may hold values from 0 to 639
- move_dst: int32 [32, 32, 4], replicated, may hold values from 0 to 639, as said below
- move_count: int32 [32, 32], replicated, may hold values from 0 to 4, as said below
- residual: bfloat16 [512, 8192], P(None, 'dp'), may hold values from -6 to 6
- out_proj: bfloat16 [8192, 8192], P('tp', 'dp'), may hold values from -1 to 1
- w_gate: bfloat16 [28672, 8192], P(('dp', 'tp')), may hold values from -0.0625 to 0.0625
- w_up: bfloat16 [28672, 8192], P(('dp', 'tp')), may hold values from -0.0625 to 0.0625
- w_down: bfloat16 [28672, 8192], P(('dp', 'tp')), may hold values from -0.15625 to 0.15625
Outputs:
- mixed: bfloat16 [512, 8192], P(None, ('dp', 'tp'))
Inputs may be any that keep to these rules, and one draw needn't show every extreme that they name: `request_block_map`: the first 512 blocks named by one rank's slots are distinct blocks of that rank's pool. `lengths`: at least one request has 512 cached tokens. `row_counts`: some rank has all 16 slots live. For a fixed destination rank e, all move_dst[s, e, c] over s and c are distinct. `move_count`: some rank receives 4 blocks from every rank.
All inputs are finite; a program needn't handle non-finite values.
Results may differ from a plain program's by a relative error of at most 0.02.
Values may be sent and summed in bfloat16 or wider, within the bound.
No kernel may reach another device: no remote copies, remote signals or barrier semaphores. Data moves between devices by JAX's collectives and lax.ppermute only.
A program may use at most 128 MiB of HBM per device.

v0:
```python
import jax
import jax.numpy as jnp
import numpy as np
from jax import lax
from jax.experimental import pallas as pl
from jax.experimental.pallas import tpu as pltpu
from jax.sharding import Mesh, PartitionSpec as P

HEAD = 128
GROUP = 8
TOKENS = 16
BF = jnp.bfloat16
F32 = jnp.float32
SCALE = np.float32(1.0) / np.sqrt(np.float32(HEAD))
NT = (((1,), (1,)), ((), ()))
NN = (((1,), (0,)), ((), ()))
REL = (0, 3, 1, 2)


def params(mib):
    return pltpu.CompilerParams(vmem_limit_bytes=mib * 2**20)


def vmem(n):
    return [pl.BlockSpec(memory_space=pltpu.VMEM)] * n


SMEM = pl.BlockSpec(memory_space=pltpu.SMEM)
ANY = pl.BlockSpec(memory_space=pl.ANY)


def weights_kernel(order_ref, gate_ref, up_ref, down_ref, own_ref, other_ref, down_own, down_other):
    order = order_ref[...]
    for j in range(gate_ref.shape[1] // 256):
        cols = slice(256 * j, 256 * j + 256)
        half = slice(128 * j, 128 * j + 128)
        for n, ref in enumerate((gate_ref, up_ref)):
            moved = lax.dot_general(ref[:, cols], order, NT, preferred_element_type=F32).astype(BF)
            rows = slice(n * moved.shape[0], (n + 1) * moved.shape[0])
            own_ref[rows, half] = moved[:, :128]
            other_ref[rows, half] = moved[:, 128:]
        moved = lax.dot_general(order, down_ref[:, cols], NT, preferred_element_type=F32).astype(BF)
        rows = moved.shape[1]
        for ref, part in ((down_own, moved[:128]), (down_other, moved[128:])):
            ref[half, :rows] = part
            ref[half, rows:] = jnp.zeros((128, ref.shape[1] - rows), BF)


def split_weights(order, w_gate, w_up, w_down):
    rows, width = w_gate.shape
    step = 1024
    half = step // 2
    return pl.pallas_call(
        weights_kernel,
        grid=(width // step,),
        in_specs=[pl.BlockSpec((256, 256), lambda i: (0, 0))]
        + [pl.BlockSpec((rows, step), lambda i: (0, i))] * 3,
        out_specs=[pl.BlockSpec((2 * rows, half), lambda i: (0, i))] * 2
        + [pl.BlockSpec((half, HEAD), lambda i: (i, 0))] * 2,
        out_shape=[jax.ShapeDtypeStruct((2 * rows, width // 2), BF)] * 2
        + [jax.ShapeDtypeStruct((width // 2, HEAD), BF)] * 2,
        compiler_params=params(58),
    )(order, w_gate, w_up, w_down)


def load_pool(pool_ref, blocks, sems):
    parts = sems.shape[0]
    rows = blocks.shape[0] // parts
    loads = [
        pltpu.make_async_copy(
            pool_ref.at[pl.ds(n * rows, rows)], blocks.at[pl.ds(n * rows, rows)], sems.at[n]
        )
        for n in range(parts)
    ]
    for load in loads:
        load.start()
    for load in loads:
        load.wait()


def parcel_kernel(source, pool_ref, out_ref, blocks, sems):
    load_pool(pool_ref, blocks, sems)

    def pick(n, carry):
        out_ref[n] = blocks[source[n]]
        return carry

    lax.fori_loop(0, out_ref.shape[0], pick, 0, unroll=8)


def parcels(source, pool):
    return pl.pallas_call(
        parcel_kernel,
        in_specs=[SMEM, ANY],
        out_specs=pl.BlockSpec(memory_space=pltpu.VMEM),
        out_shape=jax.ShapeDtypeStruct(source.shape + pool.shape[1:], BF),
        scratch_shapes=[pltpu.VMEM(pool.shape, BF), pltpu.SemaphoreType.DMA((8,))],
        compiler_params=params(58),
    )(source, pool)


def pool_kernel(
    table, q_ref, key_ref, value_ref, allowed_ref, pool_ref,
    out_ref, top_ref, total_ref, keys, values, scores,
):
    slots, depth = table.shape

    def fetch(i, carry):
        for j in range(depth):
            block = table[i, j]
            keys[i, j * TOKENS : (j + 1) * TOKENS, :] = pool_ref[block, 0]
            values[i, j * TOKENS : (j + 1) * TOKENS, :] = pool_ref[block, 1]
        return carry

    lax.fori_loop(0, slots, fetch, 0)
    for i in range(slots):
        rows = slice(i * GROUP, (i + 1) * GROUP)
        q = q_ref[rows, :]
        s = lax.dot_general(q.astype(BF), keys[i], NT, preferred_element_type=F32) * SCALE
        scores[rows, :] = jnp.where(allowed_ref[i : i + 1, :] > 0, s, F32(-1e30))
        own = jnp.sum(q * key_ref[i : i + 1, :], axis=1, keepdims=True) * SCALE
        out_ref[rows, :] = jnp.broadcast_to(own, (GROUP, HEAD))
    s = scores[...]
    own = out_ref[:, :1]
    top = jnp.maximum(jnp.max(s, axis=1, keepdims=True), own)
    e = jnp.where(s > F32(-1e29), jnp.exp(s - top), F32(0.0))
    own_e = jnp.exp(own - top)
    total = jnp.sum(e, axis=1, keepdims=True) + own_e
    scores[...] = e
    top_ref[...] = jnp.broadcast_to(top, top_ref.shape)
    total_ref[...] = jnp.broadcast_to(total, total_ref.shape)
    out_ref[...] = jnp.broadcast_to(own_e.astype(BF).astype(F32), out_ref.shape)
    for i in range(slots):
        rows = slice(i * GROUP, (i + 1) * GROUP)
        o = lax.dot_general(scores[rows, :].astype(BF), values[i], NN, preferred_element_type=F32)
        out_ref[rows, :] = o + out_ref[rows, :] * value_ref[i : i + 1, :]


def attend_pool(table, queries, fresh_key, fresh_value, allowed, pool):
    slots, depth = table.shape
    span = depth * TOKENS
    return pl.pallas_call(
        pool_kernel,
        in_specs=[SMEM] + vmem(5),
        out_specs=vmem(3),
        out_shape=[jax.ShapeDtypeStruct(queries.shape, F32)] * 3,
        scratch_shapes=[
            pltpu.VMEM((slots, span, HEAD), BF),
            pltpu.VMEM((slots, span, HEAD), BF),
            pltpu.VMEM((slots * GROUP, span), F32),
        ],
        compiler_params=params(20),
    )(table, queries, fresh_key, fresh_value, allowed, pool)


def moved_kernel(q_ref, owner_ref, arrived_ref, part_ref, top_ref, total_ref, out_ref, result):
    blocks = arrived_ref.shape[0]
    keys = arrived_ref[:, 0].reshape(blocks * TOKENS, HEAD)
    values = arrived_ref[:, 1].reshape(blocks * TOKENS, HEAD)
    s = lax.dot_general(q_ref[...].astype(BF), keys, NT, preferred_element_type=F32) * SCALE
    slot = lax.broadcasted_iota(jnp.int32, s.shape, 0) >> 3
    mine = slot == owner_ref[...]
    before = top_ref[:, :1]
    top = jnp.maximum(before, jnp.max(jnp.where(mine, s, F32(-1e30)), axis=1, keepdims=True))
    e = jnp.where(mine, jnp.exp(s - top), F32(0.0))
    keep = jnp.exp(before - top)
    total = total_ref[:, :1] * keep + jnp.sum(e, axis=1, keepdims=True)
    o = lax.dot_general(e.astype(BF), values, NN, preferred_element_type=F32)
    result[...] = (part_ref[...] * keep + o) / total
    slots = out_ref.shape[1]
    for h in range(GROUP):
        head = result[pl.ds(h, slots, stride=GROUP), :].astype(BF)
        for n in range(out_ref.shape[0]):
            out_ref[n, :, h * HEAD : (h + 1) * HEAD] = head


def attend_moved(queries, owner, arrived, part, top, total):
    slots = queries.shape[0] // GROUP
    return pl.pallas_call(
        moved_kernel,
        in_specs=vmem(6),
        out_specs=pl.BlockSpec(memory_space=pltpu.VMEM),
        out_shape=jax.ShapeDtypeStruct((8, slots, GROUP * HEAD), BF),
        scratch_shapes=[pltpu.VMEM(queries.shape, F32)],
        compiler_params=params(24),
    )(queries, owner, arrived, part, top, total)


def project_kernel(coords, rows_ref, columns_ref, out_ref, mine_ref):
    rows = rows_ref[...]
    lanes = pl.ds(pl.multiple_of(coords[0] * 128, 128), 128)
    for y in range(4):
        for part in range(2):
            at = 144 * part
            cols = lax.dot_general(
                columns_ref[y, at : at + 128, :], rows, NT, preferred_element_type=F32
            ).astype(BF)
            for n in range(4):
                out_ref[4 * part + n, 32 * y : 32 * y + 32, :] = cols[32 * n : 32 * n + 32]
            mine_ref[32 * y + 16 * part : 32 * y + 16 * part + 16, :] = columns_ref[
                y, at + 128 : at + 144, lanes
            ]


def project(coords, rows, columns):
    count = rows.shape[0]
    return pl.pallas_call(
        project_kernel,
        in_specs=[SMEM] + vmem(2),
        out_specs=vmem(2),
        out_shape=[
            jax.ShapeDtypeStruct((8, 128, count), BF),
            jax.ShapeDtypeStruct((128, count), BF),
        ],
        compiler_params=params(32),
    )(coords, rows, columns)


def up_kernel(coords, own_hbm, other_hbm, *refs):
    pieces, out_own, out_other, out_mine, stream, weights, sems = refs[:10], *refs[10:]
    rows = own_hbm.shape[0]
    loads = [
        pltpu.make_async_copy(own_hbm, weights.at[pl.ds(0, rows)], sems.at[0]),
        pltpu.make_async_copy(other_hbm, weights.at[pl.ds(rows, rows)], sems.at[1]),
    ]
    for load in loads:
        load.start()
    for part in range(2):
        own, left, right, far0, far1 = pieces[5 * part : 5 * part + 5]
        inner, outer = (0, 1) if part == 0 else (1, 0)
        for r3 in range(4):
            far = lax.rem(coords[outer] + REL[r3], 4)
            for r2 in range(4):
                near = lax.rem(coords[inner] + REL[r2], 4)
                y, x = (near, far) if part == 0 else (far, near)
                start = x * 16
                lane = pl.ds(pl.multiple_of(y * 128, 128), 128)
                for n in range(32):
                    if r3 < 3:
                        chunk = (own, left, right)[r3][r2 * 32 + n]
                    else:
                        chunk = (far0, far1)[r2 // 2][r2 % 2 * 32 + n]
                    row = (n % 4 * 8 + n // 4) * 128 + part * 64
                    stream[pl.ds(pl.multiple_of(row + start, 16), 16), lane] = chunk
    for load, out, at in zip(loads, (out_own, out_other), (0, rows)):
        load.wait()
        out[...] = lax.dot_general(
            weights[at : at + rows, :], stream[...], NN, preferred_element_type=F32
        ).reshape(out.shape)
    for part in range(2):
        row = (coords[0] * 8 + coords[2]) * 128 + part * 64 + coords[1] * 16
        out_mine[16 * part : 16 * part + 16, :] = stream[pl.ds(pl.multiple_of(row, 16), 16), :]


def gate_up(coords, own, other, pieces):
    width = 512
    return pl.pallas_call(
        up_kernel,
        in_specs=[SMEM, ANY, ANY] + vmem(10),
        out_specs=vmem(3),
        out_shape=[jax.ShapeDtypeStruct((2, own.shape[0] // 2, width), F32)] * 2
        + [jax.ShapeDtypeStruct((32, width), BF)],
        scratch_shapes=[
            pltpu.VMEM((own.shape[1], width), BF),
            pltpu.VMEM((2 * own.shape[0], own.shape[1]), BF),
            pltpu.SemaphoreType.DMA((2,)),
        ],
        compiler_params=params(48),
    )(coords, own, other, *pieces)


def chunk_of(coords, part, r3, nears, weight_refs, hidden, gathered):
    inner, outer = (0, 1) if part == 0 else (1, 0)
    far = lax.rem(coords[outer] + REL[r3], 4)
    total = None
    for ref, h in zip(weight_refs, hidden):
        for k, r2 in enumerate(nears):
            near = lax.rem(coords[inner] + REL[r2], 4)
            y, x = (near, far) if part == 0 else (far, near)
            for z in range(8):
                row = (y * 8 + z) * 128 + part * 64 + x * 16
                at = (k * 8 + z) * 16
                gathered[at : at + 16, :] = ref[pl.ds(pl.multiple_of(row, 16), 16), :]
        lhs = gathered[: len(nears) * 128, :]
        term = lax.dot_general(lhs, h, NN, preferred_element_type=F32)
        total = term if total is None else total + term
    return total.reshape(len(nears) * 8, 16, total.shape[1])


def far_kernel(coords, down_own, down_other, gu_own, gu_other, in_own, in_other, *refs):
    outs, hidden_ref, gathered = refs[:4], refs[4], refs[5]
    for n, (mine, theirs) in enumerate(((gu_own, in_own), (gu_other, in_other))):
        gate = mine[0] + theirs[0]
        up = mine[1] + theirs[1]
        rows = gate.shape[0]
        hidden_ref[n, :rows, :] = (gate * jax.nn.sigmoid(gate) * up).astype(BF)
        hidden_ref[n, rows:, :] = jnp.zeros((hidden_ref.shape[1] - rows, gate.shape[1]), BF)
    hidden = [hidden_ref[n] for n in range(2)]
    weights = (down_own, down_other)
    for part in range(2):
        for half in range(2):
            nears = (2 * half, 2 * half + 1)
            outs[2 * part + half][...] = chunk_of(
                coords, part, 3, nears, weights, hidden, gathered
            ).astype(BF)


def near_kernel(coords, down_own, down_other, hidden_ref, *refs):
    arrived, outs, gathered = refs[:4], refs[4:8], refs[8]
    hidden = [hidden_ref[n] for n in range(2)]
    weights = (down_own, down_other)
    for part in range(2):
        from_left, from_right = arrived[2 * part], arrived[2 * part + 1]
        left, right = outs[2 * part], outs[2 * part + 1]
        for r3, out, extra, half in ((1, left, from_right, 1), (2, right, from_left, 0)):
            for h in range(2):
                total = chunk_of(coords, part, r3, (2 * h, 2 * h + 1), weights, hidden, gathered)
                if h == half:
                    total = total + extra[...].astype(F32)
                out[16 * h : 16 * h + 16] = total.astype(BF)


def own_kernel(coords, down_own, down_other, hidden_ref, *refs):
    outs, gathered = refs[:2], refs[2]
    hidden = [hidden_ref[n] for n in range(2)]
    for part in range(2):
        for h in range(2):
            outs[part][16 * h : 16 * h + 16] = chunk_of(
                coords, part, 0, (2 * h, 2 * h + 1), (down_own, down_other), hidden, gathered
            ).astype(BF)


def down_call(kernel, coords, weights, extra, shapes):
    return pl.pallas_call(
        kernel,
        in_specs=[SMEM] + vmem(2 + len(extra)),
        out_specs=vmem(len(shapes)),
        out_shape=[jax.ShapeDtypeStruct(s, BF) for s in shapes],
        scratch_shapes=[pltpu.VMEM((256, weights[0].shape[1]), BF)],
        compiler_params=params(48),
    )(coords, *weights, *extra)


def finish_kernel(stream_ref, sums_ref, out_ref):
    total = stream_ref[...].astype(F32) + jnp.sum(sums_ref[...].astype(F32), axis=0)
    out_ref[...] = total.astype(BF)


def finish(stream, sums):
    return pl.pallas_call(
        finish_kernel,
        in_specs=vmem(2),
        out_specs=pl.BlockSpec(memory_space=pltpu.VMEM),
        out_shape=jax.ShapeDtypeStruct(stream.shape, BF),
        compiler_params=params(16),
    )(stream, sums)


def shift(a, axis, by):
    return lax.ppermute(a, axis, [(i, (i + by) % 4) for i in range(4)])


def direct_gather(a, axis):
    return a, shift(a, axis, 1), shift(a, axis, -1), shift(a, axis, 2)


def ring_gather(a, axis):
    half = a.shape[0] // 2
    left, right = shift(a, axis, 1), shift(a, axis, -1)
    return a, left, right, shift(left[:half], axis, 1), shift(right[half:], axis, -1)


def add(*terms):
    return sum(t.astype(F32) for t in terms).astype(BF)


def all_to_all(a, axis):
    return lax.all_to_all(a, axis, split_axis=0, concat_axis=0, tiled=True)


AXES = (("y", "x"), ("x", "y"))
SWAP = [(0, 1), (1, 0)]


def per_device(
    queries,
    fresh_token_key,
    fresh_token_value,
    key_value_pool,
    request_block_map,
    lengths,
    row_counts,
    move_src,
    move_dst,
    move_count,
    residual,
    out_proj,
    w_gate,
    w_up,
    w_down,
):
    x, y, z = lax.axis_index("x"), lax.axis_index("y"), lax.axis_index("z")
    core = lax.axis_index("core")
    rank = lax.axis_index(("y", "z"))
    group = lax.axis_index(("x", "core"))
    coords = jnp.stack([y, x, z]).astype(jnp.int32)
    ranks, _, cap = move_src.shape
    slots = queries.shape[0]

    source = lax.dynamic_index_in_dim(move_src, rank, 0, keepdims=False).reshape(-1)
    parcel = parcels(source, key_value_pool)
    parcel = parcel.reshape((ranks, cap) + key_value_pool.shape[1:])
    arrived = all_to_all(parcel, ("y", "z")).reshape((ranks * cap,) + key_value_pool.shape[1:])
    target = lax.dynamic_index_in_dim(move_dst, rank, 1, keepdims=False)
    count = lax.dynamic_index_in_dim(move_count, rank, 1, keepdims=False)
    target = jnp.where(jnp.arange(cap)[None, :] < count[:, None], target, -1).reshape(-1)
    depth = request_block_map.shape[1]
    start = jnp.arange(depth, dtype=jnp.int32) * TOKENS
    inside = jnp.clip(lengths[:, None] - start[None, :], 0, TOKENS).astype(jnp.int32)
    hit = request_block_map.reshape(1, -1) == target[:, None]
    slot_of = jnp.arange(request_block_map.size, dtype=jnp.int32) // depth
    taker = jnp.max(jnp.where(hit, slot_of[None, :], -1), axis=1)
    limit = jnp.max(jnp.where(hit, inside.reshape(1, -1), 0), axis=1)
    token = jnp.arange(TOKENS, dtype=jnp.int32)
    taker = jnp.where(token[None, :] < limit[:, None], taker[:, None], -1).reshape(1, -1)
    stays = jnp.where(jnp.any(hit, axis=0).reshape(inside.shape), 0, inside)
    allowed = (token[None, None, :] < stays[:, :, None]).astype(jnp.int32).reshape(slots, -1)

    n = np.arange(256)
    which, part, xs, j = n // 128, n // 64 % 2, n // 16 % 4, n % 16
    column = 64 * xs + 16 * part + j
    owner = jnp.where(which == 0, core, 1 - core)
    order = (jnp.arange(256)[None, :] == (column + 32 * owner)[:, None]).astype(BF)
    up_own, up_other, down_own, down_other = split_weights(order, w_gate, w_up, w_down)
    weights = (up_own, lax.ppermute(up_other, "core", SWAP))
    down_weights = (down_own, lax.ppermute(down_other, "core", SWAP))
    mine = lax.dynamic_slice_in_dim(residual, group * 32, 32, 1).T
    mine = jnp.pad(mine, ((0, 0), (0, out_proj.shape[0] - mine.shape[1])))
    columns = out_proj.T
    columns = jnp.concatenate([columns[:128], mine[:16], columns[128:], mine[16:]])
    out_weight = lax.all_gather(columns, "y")
    counts = lax.dynamic_slice_in_dim(row_counts, y * 8, 8, 0)
    live = (jnp.arange(slots)[None, :] < counts[:, None]).reshape(1, 8 * slots)

    table, up_own, down_own = lax.optimization_barrier((request_block_map, up_own, down_own))
    q = queries.reshape(slots * GROUP, HEAD).astype(F32)
    local = attend_pool(
        table, q, fresh_token_key.astype(F32), fresh_token_value.astype(F32), allowed,
        key_value_pool,
    )
    q, up_other, down_other = lax.optimization_barrier((q, weights[1], down_weights[1]))
    weights, down_weights = (up_own, up_other), (down_own, down_other)
    attended = attend_moved(q, taker, arrived, *local)
    rows = all_to_all(attended, "z").reshape(8 * slots, attended.shape[2])
    partial, mine = project(coords, rows, out_weight)
    partial = all_to_all(partial, ("x", "core"))
    piece = mine.astype(F32) + jnp.sum(partial.astype(F32), axis=0)
    piece = jnp.where(live, piece, F32(0.0)).astype(BF)
    spread = all_to_all(jnp.broadcast_to(piece[None], (8,) + piece.shape), "z")
    spread = spread.reshape(32, 2, 16, 8 * slots)
    gathered = lax.optimization_barrier(
        [direct_gather(spread[:, part], near) for part, (near, _) in enumerate(AXES)]
    )
    gathered = [jnp.concatenate(g) for g in gathered]
    pieces = []
    for part, (_, far) in enumerate(AXES):
        pieces += ring_gather(gathered[part], far)
    gu_own, gu_other, stream = gate_up(coords, *weights, pieces)
    in_other = lax.ppermute(gu_own, "core", SWAP)
    in_own = lax.ppermute(gu_other, "core", SWAP)

    width = gu_own.shape[2]
    half, whole = (16, 16, width), (32, 16, width)
    *far_sums, hidden = down_call(
        far_kernel,
        coords,
        down_weights,
        (gu_own, gu_other, in_own, in_other),
        [half] * 4 + [(2, HEAD, width)],
    )
    arriving = []
    for part, (_, far) in enumerate(AXES):
        arriving += [shift(far_sums[2 * part], far, 1), shift(far_sums[2 * part + 1], far, -1)]
    own = down_call(own_kernel, coords, down_weights, (hidden,), [whole] * 2)
    sums = down_call(near_kernel, coords, down_weights, (hidden, *arriving), [whole] * 4)
    landed = lax.optimization_barrier(
        [
            (shift(sums[2 * part + 1], far, 1), shift(sums[2 * part], far, -1))
            for part, (_, far) in enumerate(AXES)
        ]
    )
    second = []
    for part, (near, _) in enumerate(AXES):
        here, left, right, opposite = (
            add(own[part][8 * r : 8 * r + 8], *(a[8 * r : 8 * r + 8] for a in landed[part]))
            for r in range(4)
        )
        second.append(
            (here, shift(right, near, 1), shift(left, near, -1), shift(opposite, near, 2))
        )
    halves = [add(*terms) for terms in lax.optimization_barrier(second)]
    sums = all_to_all(jnp.concatenate(halves, axis=1), "z")
    return finish(stream, sums).T


def solution(mesh):
    mesh = Mesh(mesh.devices.reshape(4, 8, 4, 2), ("y", "z", "x", "core"))
    dp, tp = ("y", "z"), ("x", "core")
    return jax.shard_map(
        per_device,
        mesh=mesh,
        in_specs=(
            P(dp, tp),
            P(dp, tp),
            P(dp, tp),
            P(dp, None, None, tp),
            P(dp, None),
            P(dp),
            P(),
            P(),
            P(),
            P(),
            P(None, dp),
            P(tp, dp),
            P(dp + tp, None),
            P(dp + tp, None),
            P(dp + tp, None),
        ),
        out_specs=P(None, dp + tp),
        check_vma=False,
    )
```

profile of v0, /device:TPU:4, one launch (start us, length us, event | category | flops | bytes accessed | tf_op | source)
XLA Modules:
  0.0 215.7 jit_solution(13117483683992207378)
XLA Ops:
  7.7 1.2 copy.30
  11.3 4.4 %shard_map.164 = bf16[128,2,16,128]{3,2,1,0:T(8,128)(2,1)} custom-call(s32[128]{0:T(128)} %reshape.172.source, bf16[640,2,16,128]{3,2,1,0:T(8,128)(2,1)} %pool_ref.3), custom_call_target="tpu_custom_call" | custom-call | tf_op jit(solution)/shard_map/pallas_call | solution.py:92
  15.7 11.5 %all-to-all-start = ((bf16[32,4,2,16,128]{4,3,2,1,0:T(8,128)(2,1)}), bf16[32,4,2,16,128]{4,3,2,1,0:T(8,128)(2,1)S(1)}, u32[]{:S(2)}, u32[]{:S(2)}) async-start(bf16[32,4,2,16,128]{4,3,2,1,0:T(8,128)(2,1)} %bitcast.22), calls=%async_computation | async-start | bytes 2097152 | tf_op jit(solution)/shard_map/all_to_all | solution.py:378
  28.1 9.4 %shard_map.163 = (bf16[224,4096]{1,0:T(8,128)(2,1)}, bf16[224,4096]{1,0:T(8,128)(2,1)}, bf16[4096,128]{1,0:T(8,128)(2,1)}, bf16[4096,128]{1,0:T(8,128)(2,1)}) custom-call(bf16[256,256]{1,0:T(8,128)(2,1)} %fusion.2.order_ref, bf16[112,8192]{1,0:T(8,128)(2,1)} %gate_ref.1, bf16[112,8192]{1,0:T(8,128)(2,1)} %up_ref.1, bf16[112,8192]{1,0:T(8,128)(2,1)} %down_ref.1), custom_call_target="tpu_custom_call" | custom-call | tf_op jit(solution)/shard_map/pallas_call | solution.py:53
  40.5 2.5 %copy-done.1 = bf16[640,2,16,128]{3,2,1,0:T(8,128)(2,1)S(1)} copy-done((bf16[640,2,16,128]{3,2,1,0:T(8,128)(2,1)S(1)}, bf16[640,2,16,128]{3,2,1,0:T(8,128)(2,1)}, u32[]{:S(2)}) %copy-start.1) | copy-done | bytes 5242904
  43.1 2.2 %shard_map.165 = (f32[128,128]{1,0:T(8,128)S(1)}, f32[128,128]{1,0:T(8,128)S(1)}, f32[128,128]{1,0:T(8,128)S(1)}) custom-call(s32[16,32]{1,0:T(8,128)S(1)} %copy-done.4, f32[128,128]{1,0:T(8,128)S(1)} %reshape.178.q_ref, f32[16,128]{1,0:T(8,128)S(1)} %convert_element_type.158.key_ref, f32[16,128]{1,0:T(8,128)S(1)} %convert_element_type.159.value_ref, ...), custom_call_target="tpu_custom_call" | custom-call | tf_op jit(solution)/shard_map/pallas_call | solution.py:142
  45.3 10.6 %all-to-all-done = bf16[32,4,2,16,128]{4,3,2,1,0:T(8,128)(2,1)S(1)} async-done(((bf16[32,4,2,16,128]{4,3,2,1,0:T(8,128)(2,1)}), bf16[32,4,2,16,128]{4,3,2,1,0:T(8,128)(2,1)S(1)}, u32[]{:S(2)}, u32[]{:S(2)}) %all-to-all-start) | async-done | bytes 1048608 | tf_op jit(solution)/shard_map/all_to_all | solution.py:378
  55.9 1.7 shard_map.166
  57.6 3.9 %all-to-all-start.1 = ((bf16[8,16,1024]{2,1,0:T(8,128)(2,1)}), bf16[8,16,1024]{2,1,0:T(8,128)(2,1)S(1)}, u32[]{:S(2)}, u32[]{:S(2)}) async-start(bf16[8,16,1024]{2,1,0:T(8,128)(2,1)} %shard_map.166), calls=%async_computation.1 | async-start | bytes 524288 | tf_op jit(solution)/shard_map/all_to_all | solution.py:378
  61.6 10.4 %all-to-all-done.1 = bf16[8,16,1024]{2,1,0:T(8,128)(2,1)S(1)} async-done(((bf16[8,16,1024]{2,1,0:T(8,128)(2,1)}), bf16[8,16,1024]{2,1,0:T(8,128)(2,1)S(1)}, u32[]{:S(2)}, u32[]{:S(2)}) %all-to-all-start.1) | async-done | bytes 262176 | tf_op jit(solution)/shard_map/all_to_all | solution.py:378
  72.1 1.7 copy-done.3
  73.7 2.0 shard_map.167
  75.7 4.8 %all-to-all-start.2 = ((bf16[8,128,128]{2,1,0:T(8,128)(2,1)}), bf16[8,128,128]{2,1,0:T(8,128)(2,1)S(1)}, u32[]{:S(2)}, u32[]{:S(2)}) async-start(bf16[8,128,128]{2,1,0:T(8,128)(2,1)} %get-tuple-element.66), calls=%async_computation.2 | async-start | bytes 524288 | tf_op jit(solution)/shard_map/all_to_all | solution.py:378
  80.7 4.1 %all-to-all-done.2 = bf16[8,128,128]{2,1,0:T(8,128)(2,1)S(1)} async-done(((bf16[8,128,128]{2,1,0:T(8,128)(2,1)}), bf16[8,128,128]{2,1,0:T(8,128)(2,1)S(1)}, u32[]{:S(2)}, u32[]{:S(2)}) %all-to-all-start.2) | async-done | bytes 262176 | tf_op jit(solution)/shard_map/all_to_all | solution.py:378
  85.0 14.6 %all_to_all.25 = bf16[8,128,128]{2,1,0:T(8,128)(2,1)S(1)} all-to-all(bf16[8,128,128]{2,1,0:T(8,128)(2,1)S(1)} %broadcast_in_dim.89), channel_id=1, replica_groups=mesh['y'=4,'z'=8,'x'=4,'core'=2] {'z'}, dimensions={0} | all-to-all | bytes 524288 | tf_op jit(solution)/shard_map/all_to_all | solution.py:378
  100.7 2.2 %collective-permute-start.3 = (bf16[32,16,128]{2,1,0:T(8,128)(2,1)S(1)}, bf16[32,16,128]{2,1,0:T(8,128)(2,1)S(1)}, u32[]{:S(2)}, u32[]{:S(2)}) collective-permute-start(bf16[32,16,128]{2,1,0:T(8,128)(2,1)S(1)} %get-tuple-element.67), channel_id=1, source_target_pairs={{0,192},{64,0},{128,64},{192,128},{1,193},{65,1},{129,65},{193,129... | collective-permute-start | bytes 393224 | tf_op jit(solution)/shard_map/ppermute | solution.py:360
  104.1 1.8 collective-permute-start.5
  106.1 3.9 %collective-permute-start.7 = (bf16[32,16,128]{2,1,0:T(8,128)(2,1)S(1)}, bf16[32,16,128]{2,1,0:T(8,128)(2,1)S(1)}, u32[]{:S(2)}, u32[]{:S(2)}) collective-permute-start(bf16[32,16,128]{2,1,0:T(8,128)(2,1)S(1)} %get-tuple-element.71), channel_id=1, source_target_pairs={{0,4},{2,6},{4,0},{6,2},{1,5},{3,7},{5,1},{7,3},{8,12},{10,14},{12... | collective-permute-start | bytes 393224 | tf_op jit(solution)/shard_map/ppermute | solution.py:360
  110.9 2.1 collective-permute-done.7
  113.7 2.6 %collective-permute-start.13 = (bf16[128,16,128]{2,1,0:T(8,128)(2,1)S(1)}, bf16[128,16,128]{2,1,0:T(8,128)(2,1)S(1)}, u32[]{:S(2)}, u32[]{:S(2)}) collective-permute-start(bf16[128,16,128]{2,1,0:T(8,128)(2,1)S(1)} %constant_dynamic-update-slice_fusion.4.refs_5_), channel_id=1, source_target_pairs={{0,192},{64,0},{128,64},{192,128},{1,193},{65,1},{129,65},{193,129... | collective-permute-start | bytes 1572872 | tf_op jit(solution)/shard_map/ppermute | solution.py:360
  116.5 2.6 %collective-permute-start.8 = (bf16[128,16,128]{2,1,0:T(8,128)(2,1)S(1)}, bf16[128,16,128]{2,1,0:T(8,128)(2,1)S(1)}, u32[]{:S(2)}, u32[]{:S(2)}) collective-permute-start(bf16[128,16,128]{2,1,0:T(8,128)(2,1)S(1)} %constant_dynamic-update-slice_fusion.refs_0_), channel_id=1, source_target_pairs={{0,2},{2,4},{4,6},{6,0},{1,3},{3,5},{5,7},{7,1},{8,10},{10,12},{12... | collective-permute-start | bytes 1572872 | tf_op jit(solution)/shard_map/ppermute | solution.py:360
  119.1 6.3 %collective-permute-done.12.refs_6_ = bf16[128,16,128]{2,1,0:T(8,128)(2,1)S(1)} collective-permute-done((bf16[128,16,128]{2,1,0:T(8,128)(2,1)S(1)}, bf16[128,16,128]{2,1,0:T(8,128)(2,1)S(1)}, u32[]{:S(2)}, u32[]{:S(2)}) %collective-permute-start.12) | collective-permute-done | bytes 524320 | tf_op jit(solution)/shard_map/ppermute | solution.py:360
  125.6 3.3 %collective-permute-start.15 = (bf16[64,16,128]{2,1,0:T(8,128)(2,1)S(1)}, bf16[64,16,128]{2,1,0:T(8,128)(2,1)S(1)}, u32[]{:S(2)}, u32[]{:S(2)}) collective-permute-start(bf16[64,16,128]{2,1,0:T(8,128)(2,1)S(1)} %slice.143), channel_id=1, source_target_pairs={{0,192},{64,0},{128,64},{192,128},{1,193},{65,1},{129,65},{193,129... | collective-permute-start | bytes 786440 | tf_op jit(solution)/shard_map/ppermute | solution.py:360
  128.9 2.3 %collective-permute-start.10 = (bf16[64,16,128]{2,1,0:T(8,128)(2,1)S(1)}, bf16[64,16,128]{2,1,0:T(8,128)(2,1)S(1)}, u32[]{:S(2)}, u32[]{:S(2)}) collective-permute-start(bf16[64,16,128]{2,1,0:T(8,128)(2,1)S(1)} %slice.140), channel_id=1, source_target_pairs={{0,2},{2,4},{4,6},{6,0},{1,3},{3,5},{5,7},{7,1},{8,10},{10,12},{12... | collective-permute-start | bytes 786440 | tf_op jit(solution)/shard_map/ppermute | solution.py:360
  133.1 3.4 %collective-permute-done.10.refs_3_ = bf16[64,16,128]{2,1,0:T(8,128)(2,1)S(1)} collective-permute-done((bf16[64,16,128]{2,1,0:T(8,128)(2,1)S(1)}, bf16[64,16,128]{2,1,0:T(8,128)(2,1)S(1)}, u32[]{:S(2)}, u32[]{:S(2)}) %collective-permute-start.10) | collective-permute-done | bytes 262176 | tf_op jit(solution)/shard_map/ppermute | solution.py:360
  136.6 1.3 collective-permute-done.11.refs_4_
  137.8 5.9 %shard_map.168 = (f32[2,112,512]{2,1,0:T(8,128)S(1)}, f32[2,112,512]{2,1,0:T(8,128)S(1)}, bf16[32,512]{1,0:T(8,128)(2,1)S(1)}) custom-call(s32[3]{0:T(128)S(1)} %pad_add_fusion.coords, bf16[224,4096]{1,0:T(8,128)(2,1)} %get-tuple-element.56.own_hbm, bf16[224,4096]{1,0:T(8,128)(2,1)} %collective-permute-done.other_hbm, ...), custom_call_target="tpu_custom_call" | custom-call | tf_op jit(solution)/shard_map/pallas_call | solution.py:257
  144.3 1.3 collective-permute-done.16.in_own
  146.3 1.3 shard_map.169
  147.6 3.3 %collective-permute-start.18 = (bf16[16,16,512]{2,1,0:T(8,128)(2,1)S(1)}, bf16[16,16,512]{2,1,0:T(8,128)(2,1)S(1)}, u32[]{:S(2)}, u32[]{:S(2)}) collective-permute-start(bf16[16,16,512]{2,1,0:T(8,128)(2,1)S(1)} %get-tuple-element.82), channel_id=1, source_target_pairs={{0,2},{2,4},{4,6},{6,0},{1,3},{3,5},{5,7},{7,1},{8,10},{10,12},{12... | collective-permute-start | bytes 786440 | tf_op jit(solution)/shard_map/ppermute | solution.py:360
  150.9 3.2 %collective-permute-start.21 = (bf16[16,16,512]{2,1,0:T(8,128)(2,1)S(1)}, bf16[16,16,512]{2,1,0:T(8,128)(2,1)S(1)}, u32[]{:S(2)}, u32[]{:S(2)}) collective-permute-start(bf16[16,16,512]{2,1,0:T(8,128)(2,1)S(1)} %get-tuple-element.85), channel_id=1, source_target_pairs={{0,192},{64,0},{128,64},{192,128},{1,193},{65,1},{129,65},{193,129... | collective-permute-start | bytes 786440 | tf_op jit(solution)/shard_map/ppermute | solution.py:360
  154.2 2.6 %collective-permute-done.18.refs_0_ = bf16[16,16,512]{2,1,0:T(8,128)(2,1)S(1)} collective-permute-done((bf16[16,16,512]{2,1,0:T(8,128)(2,1)S(1)}, bf16[16,16,512]{2,1,0:T(8,128)(2,1)S(1)}, u32[]{:S(2)}, u32[]{:S(2)}) %collective-permute-start.18) | collective-permute-done | bytes 262176 | tf_op jit(solution)/shard_map/ppermute | solution.py:360
  156.8 2.2 %collective-permute-done.19.refs_1_ = bf16[16,16,512]{2,1,0:T(8,128)(2,1)S(1)} collective-permute-done((bf16[16,16,512]{2,1,0:T(8,128)(2,1)S(1)}, bf16[16,16,512]{2,1,0:T(8,128)(2,1)S(1)}, u32[]{:S(2)}, u32[]{:S(2)}) %collective-permute-start.19) | collective-permute-done | bytes 262176 | tf_op jit(solution)/shard_map/ppermute | solution.py:360
  159.0 1.2 collective-permute-done.20.refs_2_
  160.2 1.9 shard_map.171
  162.1 1.8 collective-permute-start.22
  164.2 3.2 %collective-permute-start.25 = (bf16[32,16,512]{2,1,0:T(8,128)(2,1)S(1)}, bf16[32,16,512]{2,1,0:T(8,128)(2,1)S(1)}, u32[]{:S(2)}, u32[]{:S(2)}) collective-permute-start(bf16[32,16,512]{2,1,0:T(8,128)(2,1)S(1)} %get-tuple-element.89), channel_id=1, source_target_pairs={{0,192},{64,0},{128,64},{192,128},{1,193},{65,1},{129,65},{193,129... | collective-permute-start | bytes 1572872 | tf_op jit(solution)/shard_map/ppermute | solution.py:360
  167.4 1.3 shard_map.170
  168.7 6.3 %collective-permute-done.22 = bf16[32,16,512]{2,1,0:T(8,128)(2,1)S(1)} collective-permute-done((bf16[32,16,512]{2,1,0:T(8,128)(2,1)S(1)}, bf16[32,16,512]{2,1,0:T(8,128)(2,1)S(1)}, u32[]{:S(2)}, u32[]{:S(2)}) %collective-permute-start.22) | collective-permute-done | bytes 524320 | tf_op jit(solution)/shard_map/ppermute | solution.py:360
  175.0 1.1 collective-permute-done.23
  176.1 1.5 collective-permute-done.24
  177.9 1.5 collective-permute-start.29
  180.1 4.4 %collective-permute-start.31 = (bf16[8,16,512]{2,1,0:T(8,128)(2,1)S(1)}, bf16[8,16,512]{2,1,0:T(8,128)(2,1)S(1)}, u32[]{:S(2)}, u32[]{:S(2)}) collective-permute-start(bf16[8,16,512]{2,1,0:T(8,128)(2,1)S(1)} %get-tuple-element.105), channel_id=1, source_target_pairs={{0,4},{2,6},{4,0},{6,2},{1,5},{3,7},{5,1},{7,3},{8,12},{10,14},{12... | collective-permute-start | bytes 393224 | tf_op jit(solution)/shard_map/ppermute | solution.py:360
  185.6 2.4 %collective-permute-start.27 = (bf16[8,16,512]{2,1,0:T(8,128)(2,1)S(1)}, bf16[8,16,512]{2,1,0:T(8,128)(2,1)S(1)}, u32[]{:S(2)}, u32[]{:S(2)}) collective-permute-start(bf16[8,16,512]{2,1,0:T(8,128)(2,1)S(1)} %get-tuple-element.110), channel_id=1, source_target_pairs={{0,192},{64,0},{128,64},{192,128},{1,193},{65,1},{129,65},{193,129... | collective-permute-start | bytes 393224 | tf_op jit(solution)/shard_map/ppermute | solution.py:360
  188.0 1.4 collective-permute-start.28
  189.4 1.5 collective-permute-done.26
  191.0 3.5 %collective-permute-done.28 = bf16[8,16,512]{2,1,0:T(8,128)(2,1)S(1)} collective-permute-done((bf16[8,16,512]{2,1,0:T(8,128)(2,1)S(1)}, bf16[8,16,512]{2,1,0:T(8,128)(2,1)S(1)}, u32[]{:S(2)}, u32[]{:S(2)}) %collective-permute-start.28) | collective-permute-done | bytes 131104 | tf_op jit(solution)/shard_map/ppermute | solution.py:360
  194.7 13.5 %all_to_all.26.sums_ref = bf16[8,32,512]{2,1,0:T(8,128)(2,1)S(1)} all-to-all(bf16[8,32,512]{2,1,0:T(8,128)(2,1)S(1)} %pad_maximum_fusion.1), channel_id=1, replica_groups=mesh['y'=4,'z'=8,'x'=4,'core'=2] {'z'}, dimensions={0} | all-to-all | bytes 524288 | tf_op jit(solution)/shard_map/all_to_all | solution.py:378
  (124 shorter events, 18.3 us)
Async XLA Ops:
  6.5 65.5 %all-gather.3.cloned.1.call-start = ((), (), s32[]{:S(2)}) async-start(), calls=%async_computation.5 | async-start | bytes 2949120 | tf_op jit(solution)/shard_map/all_gather | solution.py:441
  15.7 11.5 %copy-start.10 = (s32[256]{0:T(256)S(1)}, s32[256]{0:T(256)}, u32[]{:S(2)}) copy-start(s32[256]{0:T(256)} %constant.73.clone) | copy-start | bytes 3076
  15.7 11.5 %copy-start.12 = (pred[256]{0:T(512)(128)(4,1)S(1)}, pred[256]{0:T(512)(128)(4,1)}, u32[]{:S(2)}) copy-start(pred[256]{0:T(512)(128)(4,1)} %constant.72.clone) | copy-start | bytes 772
  15.7 40.2 %all-to-all-start = ((bf16[32,4,2,16,128]{4,3,2,1,0:T(8,128)(2,1)}), bf16[32,4,2,16,128]{4,3,2,1,0:T(8,128)(2,1)S(1)}, u32[]{:S(2)}, u32[]{:S(2)}) async-start(bf16[32,4,2,16,128]{4,3,2,1,0:T(8,128)(2,1)} %bitcast.22), calls=%async_computation | async-start | bytes 2097152 | tf_op jit(solution)/shard_map/all_to_all | solution.py:378
  28.1 9.9 %copy-start.5 = (s32[32,32,4]{1,2,0:T(4,128)S(1)}, s32[32,32,4]{1,2,0:T(4,128)}, u32[]{:S(2)}) copy-start(s32[32,32,4]{1,2,0:T(4,128)} %param.25) | copy-start | bytes 49156
  28.1 10.7 %copy-start.7 = (s32[32,32]{1,0:T(8,128)S(1)}, s32[32,32]{1,0:T(8,128)}, u32[]{:S(2)}) copy-start(s32[32,32]{1,0:T(8,128)} %param.26) | copy-start | bytes 12292
  28.1 11.1 %copy-start.4 = (s32[16,32]{1,0:T(8,128)S(1)}, s32[16,32]{1,0:T(8,128)}, u32[]{:S(2)}) copy-start(s32[16,32]{1,0:T(8,128)} %table) | copy-start | bytes 6148
  28.1 11.4 %copy-start.11 = (s32[16]{0:T(128)S(1)}, s32[16]{0:T(128)}, u32[]{:S(2)}) copy-start(s32[16]{0:T(128)} %param.22) | copy-start | bytes 196
  28.1 12.4 %copy-start.6 = (bf16[16,1024]{1,0:T(8,128)(2,1)S(1)}, bf16[16,1024]{1,0:T(8,128)(2,1)}, u32[]{:S(2)}) copy-start(bf16[16,1024]{1,0:T(8,128)(2,1)} %param.17) | copy-start | bytes 98308
  28.1 12.4 %copy-start.8 = (bf16[16,128]{1,0:T(8,128)(2,1)S(1)}, bf16[16,128]{1,0:T(8,128)(2,1)}, u32[]{:S(2)}) copy-start(bf16[16,128]{1,0:T(8,128)(2,1)} %param.18) | copy-start | bytes 12292
  28.1 12.4 %copy-start.9 = (bf16[16,128]{1,0:T(8,128)(2,1)S(1)}, bf16[16,128]{1,0:T(8,128)(2,1)}, u32[]{:S(2)}) copy-start(bf16[16,128]{1,0:T(8,128)(2,1)} %param.19) | copy-start | bytes 12292
  37.5 7.8 %collective-permute-start = (bf16[224,4096]{1,0:T(8,128)(2,1)}, bf16[224,4096]{1,0:T(8,128)(2,1)}, u32[]{:S(2)}, u32[]{:S(2)}) collective-permute-start(bf16[224,4096]{1,0:T(8,128)(2,1)} %get-tuple-element.57), channel_id=1, source_target_pairs={{0,1},{1,0},{2,3},{3,2},{4,5},{5,4},{6,7},{7,6},{8,9},{9,8},{10,11... | collective-permute-start | bytes 5505032 | tf_op jit(solution)/shard_map/ppermute | solution.py:435
  37.5 7.8 %collective-permute-start.1 = (bf16[4096,128]{1,0:T(8,128)(2,1)}, bf16[4096,128]{1,0:T(8,128)(2,1)S(1)}, u32[]{:S(2)}, u32[]{:S(2)}) collective-permute-start(bf16[4096,128]{1,0:T(8,128)(2,1)} %get-tuple-element.58), channel_id=1, source_target_pairs={{0,1},{1,0},{2,3},{3,2},{4,5},{5,4},{6,7},{7,6},{8,9},{9,8},{10,11... | collective-permute-start | bytes 3145736 | tf_op jit(solution)/shard_map/ppermute | solution.py:436
  40.5 2.5 %copy-start.1 = (bf16[640,2,16,128]{3,2,1,0:T(8,128)(2,1)S(1)}, bf16[640,2,16,128]{3,2,1,0:T(8,128)(2,1)}, u32[]{:S(2)}) copy-start(bf16[640,2,16,128]{3,2,1,0:T(8,128)(2,1)} %pool_ref.3) | copy-start | bytes 15728644
  57.6 22.9 %copy-start.13 = (s32[32]{0:T(128)S(1)}, s32[32]{0:T(128)}, u32[]{:S(2)}) copy-start(s32[32]{0:T(128)} %param.23) | copy-start | bytes 388
  57.6 14.4 %all-to-all-start.1 = ((bf16[8,16,1024]{2,1,0:T(8,128)(2,1)}), bf16[8,16,1024]{2,1,0:T(8,128)(2,1)S(1)}, u32[]{:S(2)}, u32[]{:S(2)}) async-start(bf16[8,16,1024]{2,1,0:T(8,128)(2,1)} %shard_map.166), calls=%async_computation.1 | async-start | bytes 524288 | tf_op jit(solution)/shard_map/all_to_all | solution.py:378
  75.7 9.2 %all-to-all-start.2 = ((bf16[8,128,128]{2,1,0:T(8,128)(2,1)}), bf16[8,128,128]{2,1,0:T(8,128)(2,1)S(1)}, u32[]{:S(2)}, u32[]{:S(2)}) async-start(bf16[8,128,128]{2,1,0:T(8,128)(2,1)} %get-tuple-element.66), calls=%async_computation.2 | async-start | bytes 524288 | tf_op jit(solution)/shard_map/all_to_all | solution.py:378
  99.6 6.4 %collective-permute-start.2 = (bf16[32,16,128]{2,1,0:T(8,128)(2,1)S(1)}, bf16[32,16,128]{2,1,0:T(8,128)(2,1)S(1)}, u32[]{:S(2)}, u32[]{:S(2)}) collective-permute-start(bf16[32,16,128]{2,1,0:T(8,128)(2,1)S(1)} %get-tuple-element.67), channel_id=1, source_target_pairs={{0,64},{64,128},{128,192},{192,0},{1,65},{65,129},{129,193},{193,1... | collective-permute-start | bytes 393224 | tf_op jit(solution)/shard_map/ppermute | solution.py:360
  100.7 9.3 %collective-permute-start.3 = (bf16[32,16,128]{2,1,0:T(8,128)(2,1)S(1)}, bf16[32,16,128]{2,1,0:T(8,128)(2,1)S(1)}, u32[]{:S(2)}, u32[]{:S(2)}) collective-permute-start(bf16[32,16,128]{2,1,0:T(8,128)(2,1)S(1)} %get-tuple-element.67), channel_id=1, source_target_pairs={{0,192},{64,0},{128,64},{192,128},{1,193},{65,1},{129,65},{193,129... | collective-permute-start | bytes 393224 | tf_op jit(solution)/shard_map/ppermute | solution.py:360
  103.0 7.1 %collective-permute-start.4 = (bf16[32,16,128]{2,1,0:T(8,128)(2,1)S(1)}, bf16[32,16,128]{2,1,0:T(8,128)(2,1)S(1)}, u32[]{:S(2)}, u32[]{:S(2)}) collective-permute-start(bf16[32,16,128]{2,1,0:T(8,128)(2,1)S(1)} %get-tuple-element.67), channel_id=1, source_target_pairs={{0,128},{64,192},{128,0},{192,64},{1,129},{65,193},{129,1},{193,65... | collective-permute-start | bytes 393224 | tf_op jit(solution)/shard_map/ppermute | solution.py:360
  104.1 6.4 %collective-permute-start.5 = (bf16[32,16,128]{2,1,0:T(8,128)(2,1)S(1)}, bf16[32,16,128]{2,1,0:T(8,128)(2,1)S(1)}, u32[]{:S(2)}, u32[]{:S(2)}) collective-permute-start(bf16[32,16,128]{2,1,0:T(8,128)(2,1)S(1)} %get-tuple-element.71), channel_id=1, source_target_pairs={{0,2},{2,4},{4,6},{6,0},{1,3},{3,5},{5,7},{7,1},{8,10},{10,12},{12... | collective-permute-start | bytes 393224 | tf_op jit(solution)/shard_map/ppermute | solution.py:360
  105.9 5.0 %collective-permute-start.6 = (bf16[32,16,128]{2,1,0:T(8,128)(2,1)S(1)}, bf16[32,16,128]{2,1,0:T(8,128)(2,1)S(1)}, u32[]{:S(2)}, u32[]{:S(2)}) collective-permute-start(bf16[32,16,128]{2,1,0:T(8,128)(2,1)S(1)} %get-tuple-element.71), channel_id=1, source_target_pairs={{0,6},{2,0},{4,2},{6,4},{1,7},{3,1},{5,3},{7,5},{8,14},{10,8},{12,... | collective-permute-start | bytes 393224 | tf_op jit(solution)/shard_map/ppermute | solution.py:360
  106.1 6.9 %collective-permute-start.7 = (bf16[32,16,128]{2,1,0:T(8,128)(2,1)S(1)}, bf16[32,16,128]{2,1,0:T(8,128)(2,1)S(1)}, u32[]{:S(2)}, u32[]{:S(2)}) collective-permute-start(bf16[32,16,128]{2,1,0:T(8,128)(2,1)S(1)} %get-tuple-element.71), channel_id=1, source_target_pairs={{0,4},{2,6},{4,0},{6,2},{1,5},{3,7},{5,1},{7,3},{8,12},{10,14},{12... | collective-permute-start | bytes 393224 | tf_op jit(solution)/shard_map/ppermute | solution.py:360
  113.0 12.4 %collective-permute-start.12 = (bf16[128,16,128]{2,1,0:T(8,128)(2,1)S(1)}, bf16[128,16,128]{2,1,0:T(8,128)(2,1)S(1)}, u32[]{:S(2)}, u32[]{:S(2)}) collective-permute-start(bf16[128,16,128]{2,1,0:T(8,128)(2,1)S(1)} %constant_dynamic-update-slice_fusion.4.refs_5_), channel_id=1, source_target_pairs={{0,64},{64,128},{128,192},{192,0},{1,65},{65,129},{129,193},{193,1... | collective-permute-start | bytes 1572872 | tf_op jit(solution)/shard_map/ppermute | solution.py:360
  113.7 11.9 %collective-permute-start.13 = (bf16[128,16,128]{2,1,0:T(8,128)(2,1)S(1)}, bf16[128,16,128]{2,1,0:T(8,128)(2,1)S(1)}, u32[]{:S(2)}, u32[]{:S(2)}) collective-permute-start(bf16[128,16,128]{2,1,0:T(8,128)(2,1)S(1)} %constant_dynamic-update-slice_fusion.4.refs_5_), channel_id=1, source_target_pairs={{0,192},{64,0},{128,64},{192,128},{1,193},{65,1},{129,65},{193,129... | collective-permute-start | bytes 1572872 | tf_op jit(solution)/shard_map/ppermute | solution.py:360
  116.5 12.4 %collective-permute-start.8 = (bf16[128,16,128]{2,1,0:T(8,128)(2,1)S(1)}, bf16[128,16,128]{2,1,0:T(8,128)(2,1)S(1)}, u32[]{:S(2)}, u32[]{:S(2)}) collective-permute-start(bf16[128,16,128]{2,1,0:T(8,128)(2,1)S(1)} %constant_dynamic-update-slice_fusion.refs_0_), channel_id=1, source_target_pairs={{0,2},{2,4},{4,6},{6,0},{1,3},{3,5},{5,7},{7,1},{8,10},{10,12},{12... | collective-permute-start | bytes 1572872 | tf_op jit(solution)/shard_map/ppermute | solution.py:360
  119.1 12.1 %collective-permute-start.9 = (bf16[128,16,128]{2,1,0:T(8,128)(2,1)S(1)}, bf16[128,16,128]{2,1,0:T(8,128)(2,1)S(1)}, u32[]{:S(2)}, u32[]{:S(2)}) collective-permute-start(bf16[128,16,128]{2,1,0:T(8,128)(2,1)S(1)} %constant_dynamic-update-slice_fusion.refs_0_), channel_id=1, source_target_pairs={{0,6},{2,0},{4,2},{6,4},{1,7},{3,1},{5,3},{7,5},{8,14},{10,8},{12,... | collective-permute-start | bytes 1572872 | tf_op jit(solution)/shard_map/ppermute | solution.py:360
  125.5 7.7 %collective-permute-start.14 = (bf16[64,16,128]{2,1,0:T(8,128)(2,1)S(1)}, bf16[64,16,128]{2,1,0:T(8,128)(2,1)S(1)}, u32[]{:S(2)}, u32[]{:S(2)}) collective-permute-start(bf16[64,16,128]{2,1,0:T(8,128)(2,1)S(1)} %slice.142), channel_id=1, source_target_pairs={{0,64},{64,128},{128,192},{192,0},{1,65},{65,129},{129,193},{193,1... | collective-permute-start | bytes 786440 | tf_op jit(solution)/shard_map/ppermute | solution.py:360
  125.6 7.5 %collective-permute-start.15 = (bf16[64,16,128]{2,1,0:T(8,128)(2,1)S(1)}, bf16[64,16,128]{2,1,0:T(8,128)(2,1)S(1)}, u32[]{:S(2)}, u32[]{:S(2)}) collective-permute-start(bf16[64,16,128]{2,1,0:T(8,128)(2,1)S(1)} %slice.143), channel_id=1, source_target_pairs={{0,192},{64,0},{128,64},{192,128},{1,193},{65,1},{129,65},{193,129... | collective-permute-start | bytes 786440 | tf_op jit(solution)/shard_map/ppermute | solution.py:360
  128.9 7.6 %collective-permute-start.10 = (bf16[64,16,128]{2,1,0:T(8,128)(2,1)S(1)}, bf16[64,16,128]{2,1,0:T(8,128)(2,1)S(1)}, u32[]{:S(2)}, u32[]{:S(2)}) collective-permute-start(bf16[64,16,128]{2,1,0:T(8,128)(2,1)S(1)} %slice.140), channel_id=1, source_target_pairs={{0,2},{2,4},{4,6},{6,0},{1,3},{3,5},{5,7},{7,1},{8,10},{10,12},{12... | collective-permute-start | bytes 786440 | tf_op jit(solution)/shard_map/ppermute | solution.py:360
  131.2 15.0 %copy-start.2 = (bf16[4096,128]{1,0:T(8,128)(2,1)S(1)}, bf16[4096,128]{1,0:T(8,128)(2,1)}, u32[]{:S(2)}) copy-start(bf16[4096,128]{1,0:T(8,128)(2,1)} %get-tuple-element.76.down_own) | copy-start | bytes 3145732
  131.3 6.6 %collective-permute-start.11 = (bf16[64,16,128]{2,1,0:T(8,128)(2,1)S(1)}, bf16[64,16,128]{2,1,0:T(8,128)(2,1)S(1)}, u32[]{:S(2)}, u32[]{:S(2)}) collective-permute-start(bf16[64,16,128]{2,1,0:T(8,128)(2,1)S(1)} %slice.141), channel_id=1, source_target_pairs={{0,6},{2,0},{4,2},{6,4},{1,7},{3,1},{5,3},{7,5},{8,14},{10,8},{12,... | collective-permute-start | bytes 786440 | tf_op jit(solution)/shard_map/ppermute | solution.py:360
  143.7 1.9 collective-permute-start.16
  143.8 2.5 %collective-permute-start.17 = (f32[2,112,512]{2,1,0:T(8,128)S(1)}, f32[2,112,512]{2,1,0:T(8,128)S(1)}, u32[]{:S(2)}, u32[]{:S(2)}) collective-permute-start(f32[2,112,512]{2,1,0:T(8,128)S(1)} %get-tuple-element.78.gu_own), channel_id=1, source_target_pairs={{0,1},{1,0},{2,3},{3,2},{4,5},{5,4},{6,7},{7,6},{8,9},{9,8},{10,11... | collective-permute-start | bytes 1376264 | tf_op jit(solution)/shard_map/ppermute | solution.py:469
  147.6 9.2 %collective-permute-start.18 = (bf16[16,16,512]{2,1,0:T(8,128)(2,1)S(1)}, bf16[16,16,512]{2,1,0:T(8,128)(2,1)S(1)}, u32[]{:S(2)}, u32[]{:S(2)}) collective-permute-start(bf16[16,16,512]{2,1,0:T(8,128)(2,1)S(1)} %get-tuple-element.82), channel_id=1, source_target_pairs={{0,2},{2,4},{4,6},{6,0},{1,3},{3,5},{5,7},{7,1},{8,10},{10,12},{12... | collective-permute-start | bytes 786440 | tf_op jit(solution)/shard_map/ppermute | solution.py:360
  150.9 8.1 %collective-permute-start.19 = (bf16[16,16,512]{2,1,0:T(8,128)(2,1)S(1)}, bf16[16,16,512]{2,1,0:T(8,128)(2,1)S(1)}, u32[]{:S(2)}, u32[]{:S(2)}) collective-permute-start(bf16[16,16,512]{2,1,0:T(8,128)(2,1)S(1)} %get-tuple-element.83), channel_id=1, source_target_pairs={{0,6},{2,0},{4,2},{6,4},{1,7},{3,1},{5,3},{7,5},{8,14},{10,8},{12,... | collective-permute-start | bytes 786440 | tf_op jit(solution)/shard_map/ppermute | solution.py:360
  150.9 9.3 %collective-permute-start.20 = (bf16[16,16,512]{2,1,0:T(8,128)(2,1)S(1)}, bf16[16,16,512]{2,1,0:T(8,128)(2,1)S(1)}, u32[]{:S(2)}, u32[]{:S(2)}) collective-permute-start(bf16[16,16,512]{2,1,0:T(8,128)(2,1)S(1)} %get-tuple-element.84), channel_id=1, source_target_pairs={{0,64},{64,128},{128,192},{192,0},{1,65},{65,129},{129,193},{193,1... | collective-permute-start | bytes 786440 | tf_op jit(solution)/shard_map/ppermute | solution.py:360
  150.9 9.3 %collective-permute-start.21 = (bf16[16,16,512]{2,1,0:T(8,128)(2,1)S(1)}, bf16[16,16,512]{2,1,0:T(8,128)(2,1)S(1)}, u32[]{:S(2)}, u32[]{:S(2)}) collective-permute-start(bf16[16,16,512]{2,1,0:T(8,128)(2,1)S(1)} %get-tuple-element.85), channel_id=1, source_target_pairs={{0,192},{64,0},{128,64},{192,128},{1,193},{65,1},{129,65},{193,129... | collective-permute-start | bytes 786440 | tf_op jit(solution)/shard_map/ppermute | solution.py:360
  162.1 12.9 %collective-permute-start.22 = (bf16[32,16,512]{2,1,0:T(8,128)(2,1)S(1)}, bf16[32,16,512]{2,1,0:T(8,128)(2,1)S(1)}, u32[]{:S(2)}, u32[]{:S(2)}) collective-permute-start(bf16[32,16,512]{2,1,0:T(8,128)(2,1)S(1)} %get-tuple-element.86), channel_id=1, source_target_pairs={{0,2},{2,4},{4,6},{6,0},{1,3},{3,5},{5,7},{7,1},{8,10},{10,12},{12... | collective-permute-start | bytes 1572872 | tf_op jit(solution)/shard_map/ppermute | solution.py:360
  163.9 12.2 %collective-permute-start.23 = (bf16[32,16,512]{2,1,0:T(8,128)(2,1)S(1)}, bf16[32,16,512]{2,1,0:T(8,128)(2,1)S(1)}, u32[]{:S(2)}, u32[]{:S(2)}) collective-permute-start(bf16[32,16,512]{2,1,0:T(8,128)(2,1)S(1)} %get-tuple-element.87), channel_id=1, source_target_pairs={{0,6},{2,0},{4,2},{6,4},{1,7},{3,1},{5,3},{7,5},{8,14},{10,8},{12,... | collective-permute-start | bytes 1572872 | tf_op jit(solution)/shard_map/ppermute | solution.py:360
  164.2 13.5 %collective-permute-start.24 = (bf16[32,16,512]{2,1,0:T(8,128)(2,1)S(1)}, bf16[32,16,512]{2,1,0:T(8,128)(2,1)S(1)}, u32[]{:S(2)}, u32[]{:S(2)}) collective-permute-start(bf16[32,16,512]{2,1,0:T(8,128)(2,1)S(1)} %get-tuple-element.88), channel_id=1, source_target_pairs={{0,64},{64,128},{128,192},{192,0},{1,65},{65,129},{129,193},{193,1... | collective-permute-start | bytes 1572872 | tf_op jit(solution)/shard_map/ppermute | solution.py:360
  164.2 13.5 %collective-permute-start.25 = (bf16[32,16,512]{2,1,0:T(8,128)(2,1)S(1)}, bf16[32,16,512]{2,1,0:T(8,128)(2,1)S(1)}, u32[]{:S(2)}, u32[]{:S(2)}) collective-permute-start(bf16[32,16,512]{2,1,0:T(8,128)(2,1)S(1)} %get-tuple-element.89), channel_id=1, source_target_pairs={{0,192},{64,0},{128,64},{192,128},{1,193},{65,1},{129,65},{193,129... | collective-permute-start | bytes 1572872 | tf_op jit(solution)/shard_map/ppermute | solution.py:360
  177.9 10.1 %collective-permute-start.29 = (bf16[8,16,512]{2,1,0:T(8,128)(2,1)S(1)}, bf16[8,16,512]{2,1,0:T(8,128)(2,1)S(1)}, u32[]{:S(2)}, u32[]{:S(2)}) collective-permute-start(bf16[8,16,512]{2,1,0:T(8,128)(2,1)S(1)} %get-tuple-element.107), channel_id=1, source_target_pairs={{0,2},{2,4},{4,6},{6,0},{1,3},{3,5},{5,7},{7,1},{8,10},{10,12},{12... | collective-permute-start | bytes 393224 | tf_op jit(solution)/shard_map/ppermute | solution.py:360
  179.4 10.0 %collective-permute-start.30 = (bf16[8,16,512]{2,1,0:T(8,128)(2,1)S(1)}, bf16[8,16,512]{2,1,0:T(8,128)(2,1)S(1)}, u32[]{:S(2)}, u32[]{:S(2)}) collective-permute-start(bf16[8,16,512]{2,1,0:T(8,128)(2,1)S(1)} %get-tuple-element.106), channel_id=1, source_target_pairs={{0,6},{2,0},{4,2},{6,4},{1,7},{3,1},{5,3},{7,5},{8,14},{10,8},{12,... | collective-permute-start | bytes 393224 | tf_op jit(solution)/shard_map/ppermute | solution.py:360
  180.1 9.4 %collective-permute-start.31 = (bf16[8,16,512]{2,1,0:T(8,128)(2,1)S(1)}, bf16[8,16,512]{2,1,0:T(8,128)(2,1)S(1)}, u32[]{:S(2)}, u32[]{:S(2)}) collective-permute-start(bf16[8,16,512]{2,1,0:T(8,128)(2,1)S(1)} %get-tuple-element.105), channel_id=1, source_target_pairs={{0,4},{2,6},{4,0},{6,2},{1,5},{3,7},{5,1},{7,3},{8,12},{10,14},{12... | collective-permute-start | bytes 393224 | tf_op jit(solution)/shard_map/ppermute | solution.py:360
  184.7 6.3 %collective-permute-start.26 = (bf16[8,16,512]{2,1,0:T(8,128)(2,1)S(1)}, bf16[8,16,512]{2,1,0:T(8,128)(2,1)S(1)}, u32[]{:S(2)}, u32[]{:S(2)}) collective-permute-start(bf16[8,16,512]{2,1,0:T(8,128)(2,1)S(1)} %get-tuple-element.111), channel_id=1, source_target_pairs={{0,64},{64,128},{128,192},{192,0},{1,65},{65,129},{129,193},{193,1... | collective-permute-start | bytes 393224 | tf_op jit(solution)/shard_map/ppermute | solution.py:360
  185.6 5.4 %collective-permute-start.27 = (bf16[8,16,512]{2,1,0:T(8,128)(2,1)S(1)}, bf16[8,16,512]{2,1,0:T(8,128)(2,1)S(1)}, u32[]{:S(2)}, u32[]{:S(2)}) collective-permute-start(bf16[8,16,512]{2,1,0:T(8,128)(2,1)S(1)} %get-tuple-element.110), channel_id=1, source_target_pairs={{0,192},{64,0},{128,64},{192,128},{1,193},{65,1},{129,65},{193,129... | collective-permute-start | bytes 393224 | tf_op jit(solution)/shard_map/ppermute | solution.py:360
  188.0 6.5 %collective-permute-start.28 = (bf16[8,16,512]{2,1,0:T(8,128)(2,1)S(1)}, bf16[8,16,512]{2,1,0:T(8,128)(2,1)S(1)}, u32[]{:S(2)}, u32[]{:S(2)}) collective-permute-start(bf16[8,16,512]{2,1,0:T(8,128)(2,1)S(1)} %get-tuple-element.109), channel_id=1, source_target_pairs={{0,128},{64,192},{128,0},{192,64},{1,129},{65,193},{129,1},{193,65... | collective-permute-start | bytes 393224 | tf_op jit(solution)/shard_map/ppermute | solution.py:360
  (2 other events, 2.6 us)
Sparse Core Ops, SparseCore 0:
  10.0 49.7 all-gather.2
where the time goes:
time: 217 us; the launch traced here: 216 us
  starting transfers between devices  67.5 us (31%)
  waiting for transfers between devices  62 us (29%)
  Pallas kernels  30.7 us (14%)
  blocking collectives  28.1 us (13%)
  between operations  13.9 us (6%)
  local copies, waits for them, and re-layouts  10.3 us (5%)
  other arithmetic  3.21 us (1%)
    ppermute x28, starting transfers between devices, shift(): return lax.ppermute(a, axis, [(i, (i + by) % 4) for i in range(4)])  46.2 us
    ppermute x28, waiting for transfers between devices, shift(): return lax.ppermute(a, axis, [(i, (i + by) % 4) for i in range(4)])  34.8 us
    all_to_all x2, blocking collectives, all_to_all(): return lax.all_to_all(a, axis, split_axis=0, concat_axis=0, tiled=True)  28.1 us
    all_to_all x3, waiting for transfers between devices, all_to_all(): return lax.all_to_all(a, axis, split_axis=0, concat_axis=0, tiled=True)  25.2 us
    all_to_all x3, starting transfers between devices, all_to_all(): return lax.all_to_all(a, axis, split_axis=0, concat_axis=0, tiled=True)  20.2 us
    pallas_call x1, Pallas kernels, split_weights(): pl.pallas_call(weights_kernel, grid=(width // step,), in_specs=[pl.BlockS...  9.36 us
    unnamed x36, local copies, waits for them, and re-layouts  6.62 us
    pallas_call x1, Pallas kernels, gate_up(): pl.pallas_call(up_kernel, in_specs=[SMEM, ANY, ANY] + vmem(10), out_specs...  5.89 us
  transfers between devices with their start and end apart: 36, of which 20 were waited for; matrix products, arithmetic and copies ran while one was open for 2% of the time, Pallas kernels for 9%

commit v1 on v0

--- a/solution.py
+++ b/solution.py
@@ -217,11 +217,10 @@
 
 
 def up_kernel(coords, own_hbm, other_hbm, *refs):
-    pieces, out_own, out_other, out_mine, stream, weights, sems = refs[:10], *refs[10:]
-    rows = own_hbm.shape[0]
+    pieces, out_own, out_other, out_mine, stream, own_ref, other_ref, sems = refs[:10], *refs[10:]
     loads = [
-        pltpu.make_async_copy(own_hbm, weights.at[pl.ds(0, rows)], sems.at[0]),
-        pltpu.make_async_copy(other_hbm, weights.at[pl.ds(rows, rows)], sems.at[1]),
+        pltpu.make_async_copy(own_hbm, own_ref, sems.at[0]),
+        pltpu.make_async_copy(other_hbm, other_ref, sems.at[1]),
     ]
     for load in loads:
         load.start()
@@ -242,11 +241,12 @@
                         chunk = (far0, far1)[r2 // 2][r2 % 2 * 32 + n]
                     row = (n % 4 * 8 + n // 4) * 128 + part * 64
                     stream[pl.ds(pl.multiple_of(row + start, 16), 16), lane] = chunk
-    for load, out, at in zip(loads, (out_own, out_other), (0, rows)):
+    s = stream[...]
+    for load, ref, out in zip(loads, (own_ref, other_ref), (out_own, out_other)):
         load.wait()
-        out[...] = lax.dot_general(
-            weights[at : at + rows, :], stream[...], NN, preferred_element_type=F32
-        ).reshape(out.shape)
+        for n in range(2):
+            rows = slice(n * out.shape[1], (n + 1) * out.shape[1])
+            out[n] = lax.dot_general(ref[rows, :], s, NN, preferred_element_type=F32)
     for part in range(2):
         row = (coords[0] * 8 + coords[2]) * 128 + part * 64 + coords[1] * 16
         out_mine[16 * part : 16 * part + 16, :] = stream[pl.ds(pl.multiple_of(row, 16), 16), :]
@@ -262,7 +262,8 @@
         + [jax.ShapeDtypeStruct((32, width), BF)],
         scratch_shapes=[
             pltpu.VMEM((own.shape[1], width), BF),
-            pltpu.VMEM((2 * own.shape[0], own.shape[1]), BF),
+            pltpu.VMEM(own.shape, BF),
+            pltpu.VMEM(own.shape, BF),
             pltpu.SemaphoreType.DMA((2,)),
         ],
         compiler_params=params(48),

time: 217 us -> 216 us (level)
  no operation moved by 1% of the time
where the time goes in v1:
time: 216 us; the launch traced here: 215 us
  starting transfers between devices  67.9 us (31%)
  waiting for transfers between devices  62 us (29%)
  Pallas kernels  29.8 us (14%)
  blocking collectives  27.9 us (13%)
  between operations  13.9 us (6%)
  local copies, waits for them, and re-layouts  10.3 us (5%)
  other arithmetic  3.21 us (1%)
    ppermute x28, starting transfers between devices, shift(): return lax.ppermute(a, axis, [(i, (i + by) % 4) for i in range(4)])  46.6 us
    ppermute x28, waiting for transfers between devices, shift(): return lax.ppermute(a, axis, [(i, (i + by) % 4) for i in range(4)])  34.9 us
    all_to_all x2, blocking collectives, all_to_all(): return lax.all_to_all(a, axis, split_axis=0, concat_axis=0, tiled=True)  27.9 us
    all_to_all x3, waiting for transfers between devices, all_to_all(): return lax.all_to_all(a, axis, split_axis=0, concat_axis=0, tiled=True)  25.2 us
    all_to_all x3, starting transfers between devices, all_to_all(): return lax.all_to_all(a, axis, split_axis=0, concat_axis=0, tiled=True)  20.2 us
    pallas_call x1, Pallas kernels, split_weights(): pl.pallas_call(weights_kernel, grid=(width // step,), in_specs=[pl.BlockS...  9.36 us
    unnamed x36, local copies, waits for them, and re-layouts  6.62 us
    pallas_call x1, Pallas kernels, gate_up(): pl.pallas_call(up_kernel, in_specs=[SMEM, ANY, ANY] + vmem(10), out_specs...  5.07 us
  transfers between devices with their start and end apart: 36, of which 20 were waited for; matrix products, arithmetic and copies ran while one was open for 2% of the time, Pallas kernels for 9%

profile of v1, /device:TPU:4, one launch (start us, length us, event | category | flops | bytes accessed | tf_op | source)
XLA Modules:
  0.0 215.1 jit_solution(7873520172397382180)
XLA Ops:
  7.7 1.2 copy.30
  11.3 4.4 %shard_map.164 = bf16[128,2,16,128]{3,2,1,0:T(8,128)(2,1)} custom-call(s32[128]{0:T(128)} %reshape.172.source, bf16[640,2,16,128]{3,2,1,0:T(8,128)(2,1)} %pool_ref.3), custom_call_target="tpu_custom_call" | custom-call | tf_op jit(solution)/shard_map/pallas_call | solution.py:92
  15.7 11.5 %all-to-all-start = ((bf16[32,4,2,16,128]{4,3,2,1,0:T(8,128)(2,1)}), bf16[32,4,2,16,128]{4,3,2,1,0:T(8,128)(2,1)S(1)}, u32[]{:S(2)}, u32[]{:S(2)}) async-start(bf16[32,4,2,16,128]{4,3,2,1,0:T(8,128)(2,1)} %bitcast.22), calls=%async_computation | async-start | bytes 2097152 | tf_op jit(solution)/shard_map/all_to_all | solution.py:379
  28.1 9.4 %shard_map.163 = (bf16[224,4096]{1,0:T(8,128)(2,1)}, bf16[224,4096]{1,0:T(8,128)(2,1)}, bf16[4096,128]{1,0:T(8,128)(2,1)}, bf16[4096,128]{1,0:T(8,128)(2,1)}) custom-call(bf16[256,256]{1,0:T(8,128)(2,1)} %fusion.2.order_ref, bf16[112,8192]{1,0:T(8,128)(2,1)} %gate_ref.1, bf16[112,8192]{1,0:T(8,128)(2,1)} %up_ref.1, bf16[112,8192]{1,0:T(8,128)(2,1)} %down_ref.1), custom_call_target="tpu_custom_call" | custom-call | tf_op jit(solution)/shard_map/pallas_call | solution.py:53
  40.5 2.5 %copy-done.1 = bf16[640,2,16,128]{3,2,1,0:T(8,128)(2,1)S(1)} copy-done((bf16[640,2,16,128]{3,2,1,0:T(8,128)(2,1)S(1)}, bf16[640,2,16,128]{3,2,1,0:T(8,128)(2,1)}, u32[]{:S(2)}) %copy-start.1) | copy-done | bytes 5242904
  43.1 2.2 %shard_map.165 = (f32[128,128]{1,0:T(8,128)S(1)}, f32[128,128]{1,0:T(8,128)S(1)}, f32[128,128]{1,0:T(8,128)S(1)}) custom-call(s32[16,32]{1,0:T(8,128)S(1)} %copy-done.4, f32[128,128]{1,0:T(8,128)S(1)} %reshape.178.q_ref, f32[16,128]{1,0:T(8,128)S(1)} %convert_element_type.158.key_ref, f32[16,128]{1,0:T(8,128)S(1)} %convert_element_type.159.value_ref, ...), custom_call_target="tpu_custom_call" | custom-call | tf_op jit(solution)/shard_map/pallas_call | solution.py:142
  45.3 10.6 %all-to-all-done = bf16[32,4,2,16,128]{4,3,2,1,0:T(8,128)(2,1)S(1)} async-done(((bf16[32,4,2,16,128]{4,3,2,1,0:T(8,128)(2,1)}), bf16[32,4,2,16,128]{4,3,2,1,0:T(8,128)(2,1)S(1)}, u32[]{:S(2)}, u32[]{:S(2)}) %all-to-all-start) | async-done | bytes 1048608 | tf_op jit(solution)/shard_map/all_to_all | solution.py:379
  55.9 1.7 shard_map.166
  57.6 3.9 %all-to-all-start.1 = ((bf16[8,16,1024]{2,1,0:T(8,128)(2,1)}), bf16[8,16,1024]{2,1,0:T(8,128)(2,1)S(1)}, u32[]{:S(2)}, u32[]{:S(2)}) async-start(bf16[8,16,1024]{2,1,0:T(8,128)(2,1)} %shard_map.166), calls=%async_computation.1 | async-start | bytes 524288 | tf_op jit(solution)/shard_map/all_to_all | solution.py:379
  61.6 10.4 %all-to-all-done.1 = bf16[8,16,1024]{2,1,0:T(8,128)(2,1)S(1)} async-done(((bf16[8,16,1024]{2,1,0:T(8,128)(2,1)}), bf16[8,16,1024]{2,1,0:T(8,128)(2,1)S(1)}, u32[]{:S(2)}, u32[]{:S(2)}) %all-to-all-start.1) | async-done | bytes 262176 | tf_op jit(solution)/shard_map/all_to_all | solution.py:379
  72.1 1.7 copy-done.3
  73.7 2.0 shard_map.167
  75.7 4.8 %all-to-all-start.2 = ((bf16[8,128,128]{2,1,0:T(8,128)(2,1)}), bf16[8,128,128]{2,1,0:T(8,128)(2,1)S(1)}, u32[]{:S(2)}, u32[]{:S(2)}) async-start(bf16[8,128,128]{2,1,0:T(8,128)(2,1)} %get-tuple-element.66), calls=%async_computation.2 | async-start | bytes 524288 | tf_op jit(solution)/shard_map/all_to_all | solution.py:379
  80.7 4.1 %all-to-all-done.2 = bf16[8,128,128]{2,1,0:T(8,128)(2,1)S(1)} async-done(((bf16[8,128,128]{2,1,0:T(8,128)(2,1)}), bf16[8,128,128]{2,1,0:T(8,128)(2,1)S(1)}, u32[]{:S(2)}, u32[]{:S(2)}) %all-to-all-start.2) | async-done | bytes 262176 | tf_op jit(solution)/shard_map/all_to_all | solution.py:379
  85.0 14.6 %all_to_all.25 = bf16[8,128,128]{2,1,0:T(8,128)(2,1)S(1)} all-to-all(bf16[8,128,128]{2,1,0:T(8,128)(2,1)S(1)} %broadcast_in_dim.89), channel_id=1, replica_groups=mesh['y'=4,'z'=8,'x'=4,'core'=2] {'z'}, dimensions={0} | all-to-all | bytes 524288 | tf_op jit(solution)/shard_map/all_to_all | solution.py:379
  100.7 2.2 %collective-permute-start.3 = (bf16[32,16,128]{2,1,0:T(8,128)(2,1)S(1)}, bf16[32,16,128]{2,1,0:T(8,128)(2,1)S(1)}, u32[]{:S(2)}, u32[]{:S(2)}) collective-permute-start(bf16[32,16,128]{2,1,0:T(8,128)(2,1)S(1)} %get-tuple-element.67), channel_id=1, source_target_pairs={{0,192},{64,0},{128,64},{192,128},{1,193},{65,1},{129,65},{193,129... | collective-permute-start | bytes 393224 | tf_op jit(solution)/shard_map/ppermute | solution.py:361
  104.1 1.8 collective-permute-start.5
  106.1 3.9 %collective-permute-start.7 = (bf16[32,16,128]{2,1,0:T(8,128)(2,1)S(1)}, bf16[32,16,128]{2,1,0:T(8,128)(2,1)S(1)}, u32[]{:S(2)}, u32[]{:S(2)}) collective-permute-start(bf16[32,16,128]{2,1,0:T(8,128)(2,1)S(1)} %get-tuple-element.71), channel_id=1, source_target_pairs={{0,4},{2,6},{4,0},{6,2},{1,5},{3,7},{5,1},{7,3},{8,12},{10,14},{12... | collective-permute-start | bytes 393224 | tf_op jit(solution)/shard_map/ppermute | solution.py:361
  110.9 2.1 collective-permute-done.7
  113.7 2.6 %collective-permute-start.13 = (bf16[128,16,128]{2,1,0:T(8,128)(2,1)S(1)}, bf16[128,16,128]{2,1,0:T(8,128)(2,1)S(1)}, u32[]{:S(2)}, u32[]{:S(2)}) collective-permute-start(bf16[128,16,128]{2,1,0:T(8,128)(2,1)S(1)} %constant_dynamic-update-slice_fusion.4.refs_5_), channel_id=1, source_target_pairs={{0,192},{64,0},{128,64},{192,128},{1,193},{65,1},{129,65},{193,129... | collective-permute-start | bytes 1572872 | tf_op jit(solution)/shard_map/ppermute | solution.py:361
  116.5 2.6 %collective-permute-start.8 = (bf16[128,16,128]{2,1,0:T(8,128)(2,1)S(1)}, bf16[128,16,128]{2,1,0:T(8,128)(2,1)S(1)}, u32[]{:S(2)}, u32[]{:S(2)}) collective-permute-start(bf16[128,16,128]{2,1,0:T(8,128)(2,1)S(1)} %constant_dynamic-update-slice_fusion.refs_0_), channel_id=1, source_target_pairs={{0,2},{2,4},{4,6},{6,0},{1,3},{3,5},{5,7},{7,1},{8,10},{10,12},{12... | collective-permute-start | bytes 1572872 | tf_op jit(solution)/shard_map/ppermute | solution.py:361
  119.1 6.3 %collective-permute-done.12.refs_6_ = bf16[128,16,128]{2,1,0:T(8,128)(2,1)S(1)} collective-permute-done((bf16[128,16,128]{2,1,0:T(8,128)(2,1)S(1)}, bf16[128,16,128]{2,1,0:T(8,128)(2,1)S(1)}, u32[]{:S(2)}, u32[]{:S(2)}) %collective-permute-start.12) | collective-permute-done | bytes 524320 | tf_op jit(solution)/shard_map/ppermute | solution.py:361
  125.6 3.3 %collective-permute-start.15 = (bf16[64,16,128]{2,1,0:T(8,128)(2,1)S(1)}, bf16[64,16,128]{2,1,0:T(8,128)(2,1)S(1)}, u32[]{:S(2)}, u32[]{:S(2)}) collective-permute-start(bf16[64,16,128]{2,1,0:T(8,128)(2,1)S(1)} %slice.143), channel_id=1, source_target_pairs={{0,192},{64,0},{128,64},{192,128},{1,193},{65,1},{129,65},{193,129... | collective-permute-start | bytes 786440 | tf_op jit(solution)/shard_map/ppermute | solution.py:361
  128.9 2.3 %collective-permute-start.10 = (bf16[64,16,128]{2,1,0:T(8,128)(2,1)S(1)}, bf16[64,16,128]{2,1,0:T(8,128)(2,1)S(1)}, u32[]{:S(2)}, u32[]{:S(2)}) collective-permute-start(bf16[64,16,128]{2,1,0:T(8,128)(2,1)S(1)} %slice.140), channel_id=1, source_target_pairs={{0,2},{2,4},{4,6},{6,0},{1,3},{3,5},{5,7},{7,1},{8,10},{10,12},{12... | collective-permute-start | bytes 786440 | tf_op jit(solution)/shard_map/ppermute | solution.py:361
  133.1 3.4 %collective-permute-done.10.refs_3_ = bf16[64,16,128]{2,1,0:T(8,128)(2,1)S(1)} collective-permute-done((bf16[64,16,128]{2,1,0:T(8,128)(2,1)S(1)}, bf16[64,16,128]{2,1,0:T(8,128)(2,1)S(1)}, u32[]{:S(2)}, u32[]{:S(2)}) %collective-permute-start.10) | collective-permute-done | bytes 262176 | tf_op jit(solution)/shard_map/ppermute | solution.py:361
  136.6 1.3 collective-permute-done.11.refs_4_
  137.8 5.1 %shard_map.168 = (f32[2,112,512]{2,1,0:T(8,128)S(1)}, f32[2,112,512]{2,1,0:T(8,128)S(1)}, bf16[32,512]{1,0:T(8,128)(2,1)S(1)}) custom-call(s32[3]{0:T(128)S(1)} %pad_add_fusion.coords, bf16[224,4096]{1,0:T(8,128)(2,1)} %get-tuple-element.56.own_hbm, bf16[224,4096]{1,0:T(8,128)(2,1)} %collective-permute-done.other_hbm, ...), custom_call_target="tpu_custom_call" | custom-call | tf_op jit(solution)/shard_map/pallas_call | solution.py:257
  143.5 1.3 collective-permute-done.16.in_own
  145.5 1.3 shard_map.169
  146.8 3.3 %collective-permute-start.18 = (bf16[16,16,512]{2,1,0:T(8,128)(2,1)S(1)}, bf16[16,16,512]{2,1,0:T(8,128)(2,1)S(1)}, u32[]{:S(2)}, u32[]{:S(2)}) collective-permute-start(bf16[16,16,512]{2,1,0:T(8,128)(2,1)S(1)} %get-tuple-element.82), channel_id=1, source_target_pairs={{0,2},{2,4},{4,6},{6,0},{1,3},{3,5},{5,7},{7,1},{8,10},{10,12},{12... | collective-permute-start | bytes 786440 | tf_op jit(solution)/shard_map/ppermute | solution.py:361
  150.1 3.2 %collective-permute-start.21 = (bf16[16,16,512]{2,1,0:T(8,128)(2,1)S(1)}, bf16[16,16,512]{2,1,0:T(8,128)(2,1)S(1)}, u32[]{:S(2)}, u32[]{:S(2)}) collective-permute-start(bf16[16,16,512]{2,1,0:T(8,128)(2,1)S(1)} %get-tuple-element.85), channel_id=1, source_target_pairs={{0,192},{64,0},{128,64},{192,128},{1,193},{65,1},{129,65},{193,129... | collective-permute-start | bytes 786440 | tf_op jit(solution)/shard_map/ppermute | solution.py:361
  153.4 2.6 %collective-permute-done.18.refs_0_ = bf16[16,16,512]{2,1,0:T(8,128)(2,1)S(1)} collective-permute-done((bf16[16,16,512]{2,1,0:T(8,128)(2,1)S(1)}, bf16[16,16,512]{2,1,0:T(8,128)(2,1)S(1)}, u32[]{:S(2)}, u32[]{:S(2)}) %collective-permute-start.18) | collective-permute-done | bytes 262176 | tf_op jit(solution)/shard_map/ppermute | solution.py:361
  156.0 2.2 %collective-permute-done.19.refs_1_ = bf16[16,16,512]{2,1,0:T(8,128)(2,1)S(1)} collective-permute-done((bf16[16,16,512]{2,1,0:T(8,128)(2,1)S(1)}, bf16[16,16,512]{2,1,0:T(8,128)(2,1)S(1)}, u32[]{:S(2)}, u32[]{:S(2)}) %collective-permute-start.19) | collective-permute-done | bytes 262176 | tf_op jit(solution)/shard_map/ppermute | solution.py:361
  158.2 1.2 collective-permute-done.20.refs_2_
  159.4 1.9 shard_map.171
  161.3 1.8 collective-permute-start.22
  163.4 3.2 %collective-permute-start.25 = (bf16[32,16,512]{2,1,0:T(8,128)(2,1)S(1)}, bf16[32,16,512]{2,1,0:T(8,128)(2,1)S(1)}, u32[]{:S(2)}, u32[]{:S(2)}) collective-permute-start(bf16[32,16,512]{2,1,0:T(8,128)(2,1)S(1)} %get-tuple-element.89), channel_id=1, source_target_pairs={{0,192},{64,0},{128,64},{192,128},{1,193},{65,1},{129,65},{193,129... | collective-permute-start | bytes 1572872 | tf_op jit(solution)/shard_map/ppermute | solution.py:361
  166.6 1.3 shard_map.170
  167.9 6.3 %collective-permute-done.22 = bf16[32,16,512]{2,1,0:T(8,128)(2,1)S(1)} collective-permute-done((bf16[32,16,512]{2,1,0:T(8,128)(2,1)S(1)}, bf16[32,16,512]{2,1,0:T(8,128)(2,1)S(1)}, u32[]{:S(2)}, u32[]{:S(2)}) %collective-permute-start.22) | collective-permute-done | bytes 524320 | tf_op jit(solution)/shard_map/ppermute | solution.py:361
  174.2 1.5 collective-permute-done.23
  175.7 1.2 collective-permute-done.24
  177.1 1.9 collective-permute-start.29
  179.2 4.8 %collective-permute-start.31 = (bf16[8,16,512]{2,1,0:T(8,128)(2,1)S(1)}, bf16[8,16,512]{2,1,0:T(8,128)(2,1)S(1)}, u32[]{:S(2)}, u32[]{:S(2)}) collective-permute-start(bf16[8,16,512]{2,1,0:T(8,128)(2,1)S(1)} %get-tuple-element.105), channel_id=1, source_target_pairs={{0,4},{2,6},{4,0},{6,2},{1,5},{3,7},{5,1},{7,3},{8,12},{10,14},{12... | collective-permute-start | bytes 393224 | tf_op jit(solution)/shard_map/ppermute | solution.py:361
  185.2 2.4 %collective-permute-start.27 = (bf16[8,16,512]{2,1,0:T(8,128)(2,1)S(1)}, bf16[8,16,512]{2,1,0:T(8,128)(2,1)S(1)}, u32[]{:S(2)}, u32[]{:S(2)}) collective-permute-start(bf16[8,16,512]{2,1,0:T(8,128)(2,1)S(1)} %get-tuple-element.110), channel_id=1, source_target_pairs={{0,192},{64,0},{128,64},{192,128},{1,193},{65,1},{129,65},{193,129... | collective-permute-start | bytes 393224 | tf_op jit(solution)/shard_map/ppermute | solution.py:361
  187.6 1.4 collective-permute-start.28
  189.0 1.6 collective-permute-done.26
  190.7 3.5 %collective-permute-done.28 = bf16[8,16,512]{2,1,0:T(8,128)(2,1)S(1)} collective-permute-done((bf16[8,16,512]{2,1,0:T(8,128)(2,1)S(1)}, bf16[8,16,512]{2,1,0:T(8,128)(2,1)S(1)}, u32[]{:S(2)}, u32[]{:S(2)}) %collective-permute-start.28) | collective-permute-done | bytes 131104 | tf_op jit(solution)/shard_map/ppermute | solution.py:361
  194.3 13.3 %all_to_all.26.sums_ref = bf16[8,32,512]{2,1,0:T(8,128)(2,1)S(1)} all-to-all(bf16[8,32,512]{2,1,0:T(8,128)(2,1)S(1)} %pad_maximum_fusion.1), channel_id=1, replica_groups=mesh['y'=4,'z'=8,'x'=4,'core'=2] {'z'}, dimensions={0} | all-to-all | bytes 524288 | tf_op jit(solution)/shard_map/all_to_all | solution.py:379
  (124 shorter events, 17.9 us)
Async XLA Ops:
  6.5 65.5 %all-gather.3.cloned.1.call-start = ((), (), s32[]{:S(2)}) async-start(), calls=%async_computation.5 | async-start | bytes 2949120 | tf_op jit(solution)/shard_map/all_gather | solution.py:442
  15.7 11.5 %copy-start.10 = (s32[256]{0:T(256)S(1)}, s32[256]{0:T(256)}, u32[]{:S(2)}) copy-start(s32[256]{0:T(256)} %constant.73.clone) | copy-start | bytes 3076
  15.7 11.5 %copy-start.12 = (pred[256]{0:T(512)(128)(4,1)S(1)}, pred[256]{0:T(512)(128)(4,1)}, u32[]{:S(2)}) copy-start(pred[256]{0:T(512)(128)(4,1)} %constant.72.clone) | copy-start | bytes 772
  15.7 40.2 %all-to-all-start = ((bf16[32,4,2,16,128]{4,3,2,1,0:T(8,128)(2,1)}), bf16[32,4,2,16,128]{4,3,2,1,0:T(8,128)(2,1)S(1)}, u32[]{:S(2)}, u32[]{:S(2)}) async-start(bf16[32,4,2,16,128]{4,3,2,1,0:T(8,128)(2,1)} %bitcast.22), calls=%async_computation | async-start | bytes 2097152 | tf_op jit(solution)/shard_map/all_to_all | solution.py:379
  28.1 9.9 %copy-start.5 = (s32[32,32,4]{1,2,0:T(4,128)S(1)}, s32[32,32,4]{1,2,0:T(4,128)}, u32[]{:S(2)}) copy-start(s32[32,32,4]{1,2,0:T(4,128)} %param.25) | copy-start | bytes 49156
  28.1 10.7 %copy-start.7 = (s32[32,32]{1,0:T(8,128)S(1)}, s32[32,32]{1,0:T(8,128)}, u32[]{:S(2)}) copy-start(s32[32,32]{1,0:T(8,128)} %param.26) | copy-start | bytes 12292
  28.1 11.1 %copy-start.4 = (s32[16,32]{1,0:T(8,128)S(1)}, s32[16,32]{1,0:T(8,128)}, u32[]{:S(2)}) copy-start(s32[16,32]{1,0:T(8,128)} %table) | copy-start | bytes 6148
  28.1 11.4 %copy-start.11 = (s32[16]{0:T(128)S(1)}, s32[16]{0:T(128)}, u32[]{:S(2)}) copy-start(s32[16]{0:T(128)} %param.22) | copy-start | bytes 196
  28.1 12.4 %copy-start.6 = (bf16[16,1024]{1,0:T(8,128)(2,1)S(1)}, bf16[16,1024]{1,0:T(8,128)(2,1)}, u32[]{:S(2)}) copy-start(bf16[16,1024]{1,0:T(8,128)(2,1)} %param.17) | copy-start | bytes 98308
  28.1 12.4 %copy-start.8 = (bf16[16,128]{1,0:T(8,128)(2,1)S(1)}, bf16[16,128]{1,0:T(8,128)(2,1)}, u32[]{:S(2)}) copy-start(bf16[16,128]{1,0:T(8,128)(2,1)} %param.18) | copy-start | bytes 12292
  28.1 12.4 %copy-start.9 = (bf16[16,128]{1,0:T(8,128)(2,1)S(1)}, bf16[16,128]{1,0:T(8,128)(2,1)}, u32[]{:S(2)}) copy-start(bf16[16,128]{1,0:T(8,128)(2,1)} %param.19) | copy-start | bytes 12292
  37.5 7.8 %collective-permute-start = (bf16[224,4096]{1,0:T(8,128)(2,1)}, bf16[224,4096]{1,0:T(8,128)(2,1)}, u32[]{:S(2)}, u32[]{:S(2)}) collective-permute-start(bf16[224,4096]{1,0:T(8,128)(2,1)} %get-tuple-element.57), channel_id=1, source_target_pairs={{0,1},{1,0},{2,3},{3,2},{4,5},{5,4},{6,7},{7,6},{8,9},{9,8},{10,11... | collective-permute-start | bytes 5505032 | tf_op jit(solution)/shard_map/ppermute | solution.py:436
  37.5 7.8 %collective-permute-start.1 = (bf16[4096,128]{1,0:T(8,128)(2,1)}, bf16[4096,128]{1,0:T(8,128)(2,1)S(1)}, u32[]{:S(2)}, u32[]{:S(2)}) collective-permute-start(bf16[4096,128]{1,0:T(8,128)(2,1)} %get-tuple-element.58), channel_id=1, source_target_pairs={{0,1},{1,0},{2,3},{3,2},{4,5},{5,4},{6,7},{7,6},{8,9},{9,8},{10,11... | collective-permute-start | bytes 3145736 | tf_op jit(solution)/shard_map/ppermute | solution.py:437
  40.5 2.5 %copy-start.1 = (bf16[640,2,16,128]{3,2,1,0:T(8,128)(2,1)S(1)}, bf16[640,2,16,128]{3,2,1,0:T(8,128)(2,1)}, u32[]{:S(2)}) copy-start(bf16[640,2,16,128]{3,2,1,0:T(8,128)(2,1)} %pool_ref.3) | copy-start | bytes 15728644
  57.6 22.9 %copy-start.13 = (s32[32]{0:T(128)S(1)}, s32[32]{0:T(128)}, u32[]{:S(2)}) copy-start(s32[32]{0:T(128)} %param.23) | copy-start | bytes 388
  57.6 14.4 %all-to-all-start.1 = ((bf16[8,16,1024]{2,1,0:T(8,128)(2,1)}), bf16[8,16,1024]{2,1,0:T(8,128)(2,1)S(1)}, u32[]{:S(2)}, u32[]{:S(2)}) async-start(bf16[8,16,1024]{2,1,0:T(8,128)(2,1)} %shard_map.166), calls=%async_computation.1 | async-start | bytes 524288 | tf_op jit(solution)/shard_map/all_to_all | solution.py:379
  75.7 9.2 %all-to-all-start.2 = ((bf16[8,128,128]{2,1,0:T(8,128)(2,1)}), bf16[8,128,128]{2,1,0:T(8,128)(2,1)S(1)}, u32[]{:S(2)}, u32[]{:S(2)}) async-start(bf16[8,128,128]{2,1,0:T(8,128)(2,1)} %get-tuple-element.66), calls=%async_computation.2 | async-start | bytes 524288 | tf_op jit(solution)/shard_map/all_to_all | solution.py:379
  99.6 6.4 %collective-permute-start.2 = (bf16[32,16,128]{2,1,0:T(8,128)(2,1)S(1)}, bf16[32,16,128]{2,1,0:T(8,128)(2,1)S(1)}, u32[]{:S(2)}, u32[]{:S(2)}) collective-permute-start(bf16[32,16,128]{2,1,0:T(8,128)(2,1)S(1)} %get-tuple-element.67), channel_id=1, source_target_pairs={{0,64},{64,128},{128,192},{192,0},{1,65},{65,129},{129,193},{193,1... | collective-permute-start | bytes 393224 | tf_op jit(solution)/shard_map/ppermute | solution.py:361
  100.7 9.3 %collective-permute-start.3 = (bf16[32,16,128]{2,1,0:T(8,128)(2,1)S(1)}, bf16[32,16,128]{2,1,0:T(8,128)(2,1)S(1)}, u32[]{:S(2)}, u32[]{:S(2)}) collective-permute-start(bf16[32,16,128]{2,1,0:T(8,128)(2,1)S(1)} %get-tuple-element.67), channel_id=1, source_target_pairs={{0,192},{64,0},{128,64},{192,128},{1,193},{65,1},{129,65},{193,129... | collective-permute-start | bytes 393224 | tf_op jit(solution)/shard_map/ppermute | solution.py:361
  103.0 7.1 %collective-permute-start.4 = (bf16[32,16,128]{2,1,0:T(8,128)(2,1)S(1)}, bf16[32,16,128]{2,1,0:T(8,128)(2,1)S(1)}, u32[]{:S(2)}, u32[]{:S(2)}) collective-permute-start(bf16[32,16,128]{2,1,0:T(8,128)(2,1)S(1)} %get-tuple-element.67), channel_id=1, source_target_pairs={{0,128},{64,192},{128,0},{192,64},{1,129},{65,193},{129,1},{193,65... | collective-permute-start | bytes 393224 | tf_op jit(solution)/shard_map/ppermute | solution.py:361
  104.1 6.4 %collective-permute-start.5 = (bf16[32,16,128]{2,1,0:T(8,128)(2,1)S(1)}, bf16[32,16,128]{2,1,0:T(8,128)(2,1)S(1)}, u32[]{:S(2)}, u32[]{:S(2)}) collective-permute-start(bf16[32,16,128]{2,1,0:T(8,128)(2,1)S(1)} %get-tuple-element.71), channel_id=1, source_target_pairs={{0,2},{2,4},{4,6},{6,0},{1,3},{3,5},{5,7},{7,1},{8,10},{10,12},{12... | collective-permute-start | bytes 393224 | tf_op jit(solution)/shard_map/ppermute | solution.py:361
  105.9 5.0 %collective-permute-start.6 = (bf16[32,16,128]{2,1,0:T(8,128)(2,1)S(1)}, bf16[32,16,128]{2,1,0:T(8,128)(2,1)S(1)}, u32[]{:S(2)}, u32[]{:S(2)}) collective-permute-start(bf16[32,16,128]{2,1,0:T(8,128)(2,1)S(1)} %get-tuple-element.71), channel_id=1, source_target_pairs={{0,6},{2,0},{4,2},{6,4},{1,7},{3,1},{5,3},{7,5},{8,14},{10,8},{12,... | collective-permute-start | bytes 393224 | tf_op jit(solution)/shard_map/ppermute | solution.py:361
  106.1 6.9 %collective-permute-start.7 = (bf16[32,16,128]{2,1,0:T(8,128)(2,1)S(1)}, bf16[32,16,128]{2,1,0:T(8,128)(2,1)S(1)}, u32[]{:S(2)}, u32[]{:S(2)}) collective-permute-start(bf16[32,16,128]{2,1,0:T(8,128)(2,1)S(1)} %get-tuple-element.71), channel_id=1, source_target_pairs={{0,4},{2,6},{4,0},{6,2},{1,5},{3,7},{5,1},{7,3},{8,12},{10,14},{12... | collective-permute-start | bytes 393224 | tf_op jit(solution)/shard_map/ppermute | solution.py:361
  113.0 12.4 %collective-permute-start.12 = (bf16[128,16,128]{2,1,0:T(8,128)(2,1)S(1)}, bf16[128,16,128]{2,1,0:T(8,128)(2,1)S(1)}, u32[]{:S(2)}, u32[]{:S(2)}) collective-permute-start(bf16[128,16,128]{2,1,0:T(8,128)(2,1)S(1)} %constant_dynamic-update-slice_fusion.4.refs_5_), channel_id=1, source_target_pairs={{0,64},{64,128},{128,192},{192,0},{1,65},{65,129},{129,193},{193,1... | collective-permute-start | bytes 1572872 | tf_op jit(solution)/shard_map/ppermute | solution.py:361
  113.7 11.9 %collective-permute-start.13 = (bf16[128,16,128]{2,1,0:T(8,128)(2,1)S(1)}, bf16[128,16,128]{2,1,0:T(8,128)(2,1)S(1)}, u32[]{:S(2)}, u32[]{:S(2)}) collective-permute-start(bf16[128,16,128]{2,1,0:T(8,128)(2,1)S(1)} %constant_dynamic-update-slice_fusion.4.refs_5_), channel_id=1, source_target_pairs={{0,192},{64,0},{128,64},{192,128},{1,193},{65,1},{129,65},{193,129... | collective-permute-start | bytes 1572872 | tf_op jit(solution)/shard_map/ppermute | solution.py:361
  116.5 12.4 %collective-permute-start.8 = (bf16[128,16,128]{2,1,0:T(8,128)(2,1)S(1)}, bf16[128,16,128]{2,1,0:T(8,128)(2,1)S(1)}, u32[]{:S(2)}, u32[]{:S(2)}) collective-permute-start(bf16[128,16,128]{2,1,0:T(8,128)(2,1)S(1)} %constant_dynamic-update-slice_fusion.refs_0_), channel_id=1, source_target_pairs={{0,2},{2,4},{4,6},{6,0},{1,3},{3,5},{5,7},{7,1},{8,10},{10,12},{12... | collective-permute-start | bytes 1572872 | tf_op jit(solution)/shard_map/ppermute | solution.py:361
  119.1 12.1 %collective-permute-start.9 = (bf16[128,16,128]{2,1,0:T(8,128)(2,1)S(1)}, bf16[128,16,128]{2,1,0:T(8,128)(2,1)S(1)}, u32[]{:S(2)}, u32[]{:S(2)}) collective-permute-start(bf16[128,16,128]{2,1,0:T(8,128)(2,1)S(1)} %constant_dynamic-update-slice_fusion.refs_0_), channel_id=1, source_target_pairs={{0,6},{2,0},{4,2},{6,4},{1,7},{3,1},{5,3},{7,5},{8,14},{10,8},{12,... | collective-permute-start | bytes 1572872 | tf_op jit(solution)/shard_map/ppermute | solution.py:361
  125.5 7.7 %collective-permute-start.14 = (bf16[64,16,128]{2,1,0:T(8,128)(2,1)S(1)}, bf16[64,16,128]{2,1,0:T(8,128)(2,1)S(1)}, u32[]{:S(2)}, u32[]{:S(2)}) collective-permute-start(bf16[64,16,128]{2,1,0:T(8,128)(2,1)S(1)} %slice.142), channel_id=1, source_target_pairs={{0,64},{64,128},{128,192},{192,0},{1,65},{65,129},{129,193},{193,1... | collective-permute-start | bytes 786440 | tf_op jit(solution)/shard_map/ppermute | solution.py:361
  125.6 7.5 %collective-permute-start.15 = (bf16[64,16,128]{2,1,0:T(8,128)(2,1)S(1)}, bf16[64,16,128]{2,1,0:T(8,128)(2,1)S(1)}, u32[]{:S(2)}, u32[]{:S(2)}) collective-permute-start(bf16[64,16,128]{2,1,0:T(8,128)(2,1)S(1)} %slice.143), channel_id=1, source_target_pairs={{0,192},{64,0},{128,64},{192,128},{1,193},{65,1},{129,65},{193,129... | collective-permute-start | bytes 786440 | tf_op jit(solution)/shard_map/ppermute | solution.py:361
  128.9 7.6 %collective-permute-start.10 = (bf16[64,16,128]{2,1,0:T(8,128)(2,1)S(1)}, bf16[64,16,128]{2,1,0:T(8,128)(2,1)S(1)}, u32[]{:S(2)}, u32[]{:S(2)}) collective-permute-start(bf16[64,16,128]{2,1,0:T(8,128)(2,1)S(1)} %slice.140), channel_id=1, source_target_pairs={{0,2},{2,4},{4,6},{6,0},{1,3},{3,5},{5,7},{7,1},{8,10},{10,12},{12... | collective-permute-start | bytes 786440 | tf_op jit(solution)/shard_map/ppermute | solution.py:361
  131.2 14.2 %copy-start.2 = (bf16[4096,128]{1,0:T(8,128)(2,1)S(1)}, bf16[4096,128]{1,0:T(8,128)(2,1)}, u32[]{:S(2)}) copy-start(bf16[4096,128]{1,0:T(8,128)(2,1)} %get-tuple-element.76.down_own) | copy-start | bytes 3145732
  131.3 6.6 %collective-permute-start.11 = (bf16[64,16,128]{2,1,0:T(8,128)(2,1)S(1)}, bf16[64,16,128]{2,1,0:T(8,128)(2,1)S(1)}, u32[]{:S(2)}, u32[]{:S(2)}) collective-permute-start(bf16[64,16,128]{2,1,0:T(8,128)(2,1)S(1)} %slice.141), channel_id=1, source_target_pairs={{0,6},{2,0},{4,2},{6,4},{1,7},{3,1},{5,3},{7,5},{8,14},{10,8},{12,... | collective-permute-start | bytes 786440 | tf_op jit(solution)/shard_map/ppermute | solution.py:361
  142.9 1.9 collective-permute-start.16
  143.0 2.5 %collective-permute-start.17 = (f32[2,112,512]{2,1,0:T(8,128)S(1)}, f32[2,112,512]{2,1,0:T(8,128)S(1)}, u32[]{:S(2)}, u32[]{:S(2)}) collective-permute-start(f32[2,112,512]{2,1,0:T(8,128)S(1)} %get-tuple-element.78.gu_own), channel_id=1, source_target_pairs={{0,1},{1,0},{2,3},{3,2},{4,5},{5,4},{6,7},{7,6},{8,9},{9,8},{10,11... | collective-permute-start | bytes 1376264 | tf_op jit(solution)/shard_map/ppermute | solution.py:470
  146.8 9.2 %collective-permute-start.18 = (bf16[16,16,512]{2,1,0:T(8,128)(2,1)S(1)}, bf16[16,16,512]{2,1,0:T(8,128)(2,1)S(1)}, u32[]{:S(2)}, u32[]{:S(2)}) collective-permute-start(bf16[16,16,512]{2,1,0:T(8,128)(2,1)S(1)} %get-tuple-element.82), channel_id=1, source_target_pairs={{0,2},{2,4},{4,6},{6,0},{1,3},{3,5},{5,7},{7,1},{8,10},{10,12},{12... | collective-permute-start | bytes 786440 | tf_op jit(solution)/shard_map/ppermute | solution.py:361
  150.1 8.1 %collective-permute-start.19 = (bf16[16,16,512]{2,1,0:T(8,128)(2,1)S(1)}, bf16[16,16,512]{2,1,0:T(8,128)(2,1)S(1)}, u32[]{:S(2)}, u32[]{:S(2)}) collective-permute-start(bf16[16,16,512]{2,1,0:T(8,128)(2,1)S(1)} %get-tuple-element.83), channel_id=1, source_target_pairs={{0,6},{2,0},{4,2},{6,4},{1,7},{3,1},{5,3},{7,5},{8,14},{10,8},{12,... | collective-permute-start | bytes 786440 | tf_op jit(solution)/shard_map/ppermute | solution.py:361
  150.1 9.3 %collective-permute-start.20 = (bf16[16,16,512]{2,1,0:T(8,128)(2,1)S(1)}, bf16[16,16,512]{2,1,0:T(8,128)(2,1)S(1)}, u32[]{:S(2)}, u32[]{:S(2)}) collective-permute-start(bf16[16,16,512]{2,1,0:T(8,128)(2,1)S(1)} %get-tuple-element.84), channel_id=1, source_target_pairs={{0,64},{64,128},{128,192},{192,0},{1,65},{65,129},{129,193},{193,1... | collective-permute-start | bytes 786440 | tf_op jit(solution)/shard_map/ppermute | solution.py:361
  150.1 9.3 %collective-permute-start.21 = (bf16[16,16,512]{2,1,0:T(8,128)(2,1)S(1)}, bf16[16,16,512]{2,1,0:T(8,128)(2,1)S(1)}, u32[]{:S(2)}, u32[]{:S(2)}) collective-permute-start(bf16[16,16,512]{2,1,0:T(8,128)(2,1)S(1)} %get-tuple-element.85), channel_id=1, source_target_pairs={{0,192},{64,0},{128,64},{192,128},{1,193},{65,1},{129,65},{193,129... | collective-permute-start | bytes 786440 | tf_op jit(solution)/shard_map/ppermute | solution.py:361
  161.3 12.9 %collective-permute-start.22 = (bf16[32,16,512]{2,1,0:T(8,128)(2,1)S(1)}, bf16[32,16,512]{2,1,0:T(8,128)(2,1)S(1)}, u32[]{:S(2)}, u32[]{:S(2)}) collective-permute-start(bf16[32,16,512]{2,1,0:T(8,128)(2,1)S(1)} %get-tuple-element.86), channel_id=1, source_target_pairs={{0,2},{2,4},{4,6},{6,0},{1,3},{3,5},{5,7},{7,1},{8,10},{10,12},{12... | collective-permute-start | bytes 1572872 | tf_op jit(solution)/shard_map/ppermute | solution.py:361
  163.1 12.6 %collective-permute-start.23 = (bf16[32,16,512]{2,1,0:T(8,128)(2,1)S(1)}, bf16[32,16,512]{2,1,0:T(8,128)(2,1)S(1)}, u32[]{:S(2)}, u32[]{:S(2)}) collective-permute-start(bf16[32,16,512]{2,1,0:T(8,128)(2,1)S(1)} %get-tuple-element.87), channel_id=1, source_target_pairs={{0,6},{2,0},{4,2},{6,4},{1,7},{3,1},{5,3},{7,5},{8,14},{10,8},{12,... | collective-permute-start | bytes 1572872 | tf_op jit(solution)/shard_map/ppermute | solution.py:361
  163.4 13.5 %collective-permute-start.24 = (bf16[32,16,512]{2,1,0:T(8,128)(2,1)S(1)}, bf16[32,16,512]{2,1,0:T(8,128)(2,1)S(1)}, u32[]{:S(2)}, u32[]{:S(2)}) collective-permute-start(bf16[32,16,512]{2,1,0:T(8,128)(2,1)S(1)} %get-tuple-element.88), channel_id=1, source_target_pairs={{0,64},{64,128},{128,192},{192,0},{1,65},{65,129},{129,193},{193,1... | collective-permute-start | bytes 1572872 | tf_op jit(solution)/shard_map/ppermute | solution.py:361
  163.4 13.5 %collective-permute-start.25 = (bf16[32,16,512]{2,1,0:T(8,128)(2,1)S(1)}, bf16[32,16,512]{2,1,0:T(8,128)(2,1)S(1)}, u32[]{:S(2)}, u32[]{:S(2)}) collective-permute-start(bf16[32,16,512]{2,1,0:T(8,128)(2,1)S(1)} %get-tuple-element.89), channel_id=1, source_target_pairs={{0,192},{64,0},{128,64},{192,128},{1,193},{65,1},{129,65},{193,129... | collective-permute-start | bytes 1572872 | tf_op jit(solution)/shard_map/ppermute | solution.py:361
  177.1 10.5 %collective-permute-start.29 = (bf16[8,16,512]{2,1,0:T(8,128)(2,1)S(1)}, bf16[8,16,512]{2,1,0:T(8,128)(2,1)S(1)}, u32[]{:S(2)}, u32[]{:S(2)}) collective-permute-start(bf16[8,16,512]{2,1,0:T(8,128)(2,1)S(1)} %get-tuple-element.107), channel_id=1, source_target_pairs={{0,2},{2,4},{4,6},{6,0},{1,3},{3,5},{5,7},{7,1},{8,10},{10,12},{12... | collective-permute-start | bytes 393224 | tf_op jit(solution)/shard_map/ppermute | solution.py:361
  179.0 10.0 %collective-permute-start.30 = (bf16[8,16,512]{2,1,0:T(8,128)(2,1)S(1)}, bf16[8,16,512]{2,1,0:T(8,128)(2,1)S(1)}, u32[]{:S(2)}, u32[]{:S(2)}) collective-permute-start(bf16[8,16,512]{2,1,0:T(8,128)(2,1)S(1)} %get-tuple-element.106), channel_id=1, source_target_pairs={{0,6},{2,0},{4,2},{6,4},{1,7},{3,1},{5,3},{7,5},{8,14},{10,8},{12,... | collective-permute-start | bytes 393224 | tf_op jit(solution)/shard_map/ppermute | solution.py:361
  179.2 9.8 %collective-permute-start.31 = (bf16[8,16,512]{2,1,0:T(8,128)(2,1)S(1)}, bf16[8,16,512]{2,1,0:T(8,128)(2,1)S(1)}, u32[]{:S(2)}, u32[]{:S(2)}) collective-permute-start(bf16[8,16,512]{2,1,0:T(8,128)(2,1)S(1)} %get-tuple-element.105), channel_id=1, source_target_pairs={{0,4},{2,6},{4,0},{6,2},{1,5},{3,7},{5,1},{7,3},{8,12},{10,14},{12... | collective-permute-start | bytes 393224 | tf_op jit(solution)/shard_map/ppermute | solution.py:361
  184.3 6.3 %collective-permute-start.26 = (bf16[8,16,512]{2,1,0:T(8,128)(2,1)S(1)}, bf16[8,16,512]{2,1,0:T(8,128)(2,1)S(1)}, u32[]{:S(2)}, u32[]{:S(2)}) collective-permute-start(bf16[8,16,512]{2,1,0:T(8,128)(2,1)S(1)} %get-tuple-element.111), channel_id=1, source_target_pairs={{0,64},{64,128},{128,192},{192,0},{1,65},{65,129},{129,193},{193,1... | collective-permute-start | bytes 393224 | tf_op jit(solution)/shard_map/ppermute | solution.py:361
  185.2 5.4 %collective-permute-start.27 = (bf16[8,16,512]{2,1,0:T(8,128)(2,1)S(1)}, bf16[8,16,512]{2,1,0:T(8,128)(2,1)S(1)}, u32[]{:S(2)}, u32[]{:S(2)}) collective-permute-start(bf16[8,16,512]{2,1,0:T(8,128)(2,1)S(1)} %get-tuple-element.110), channel_id=1, source_target_pairs={{0,192},{64,0},{128,64},{192,128},{1,193},{65,1},{129,65},{193,129... | collective-permute-start | bytes 393224 | tf_op jit(solution)/shard_map/ppermute | solution.py:361
  187.6 6.5 %collective-permute-start.28 = (bf16[8,16,512]{2,1,0:T(8,128)(2,1)S(1)}, bf16[8,16,512]{2,1,0:T(8,128)(2,1)S(1)}, u32[]{:S(2)}, u32[]{:S(2)}) collective-permute-start(bf16[8,16,512]{2,1,0:T(8,128)(2,1)S(1)} %get-tuple-element.109), channel_id=1, source_target_pairs={{0,128},{64,192},{128,0},{192,64},{1,129},{65,193},{129,1},{193,65... | collective-permute-start | bytes 393224 | tf_op jit(solution)/shard_map/ppermute | solution.py:361
  (2 other events, 2.6 us)
Sparse Core Ops, SparseCore 0:
  10.0 49.7 all-gather.2
